TPU v7x, 32 devices: a whole 2x2x4 slice. The times are simulated.
32 devices in a mesh: row: 8 (over y, x, core), col: 4 (over z).
Axes of the slice: x: 2, y: 2, z: 4, core: 2. Of those that a mesh axis runs over, the one named last changes fastest.
Arguments:
- trial: float32 [1, 256, 1024], P(None, None, 'row'), may hold values from -6 to 6
- screened: bfloat16 [768, 768], P('row', 'col'), may hold values from -4 to 4
- val_points: bfloat16 [768, 256], P('row'), may hold values from -0.375 to 0.375
- cond_points: bfloat16 [768, 1024], P('col', 'row'), may hold values from -0.1875 to 0.1875
- eps_val: float32 [256], replicated, may hold values from -0.6 to -0.1
- eps_cond: float32 [1024], replicated, may hold values from 0.1 to 1
Outputs:
- applied: float32 [1, 256, 1024], P(None, None, 'row')
All inputs are finite; a program needn't handle non-finite values.
Results may differ from a plain program's by a relative error of at most 0.02.
Values may be sent and summed in bfloat16 or wider, within the bound.
A program may use at most 64 MiB of HBM per device.

v0:
```python
import jax
import jax.numpy as jnp
from jax import lax
from jax.sharding import PartitionSpec as P

APPLY = 2


def body(trial, screened, val_points, cond_points, eps_val, eps_cond):
    cond_full = lax.all_gather(cond_points, "row", axis=1, tiled=True)
    energy_full = eps_cond[None, :] - eps_val[:, None]
    width = trial.shape[2]
    offset = lax.axis_index("row") * width
    x_full = lax.all_gather(trial.astype(jnp.bfloat16), "row", axis=2, tiled=True).astype(
        trial.dtype
    )
    xb_full = x_full.astype(jnp.bfloat16)
    x_mine = trial
    for step in range(APPLY):
        pair = jnp.einsum(
            "mv,bvc->bmc", val_points, xb_full, preferred_element_type=jnp.float32
        ).astype(jnp.bfloat16)
        inner = jnp.einsum("bmc,nc->bmn", pair, cond_full, preferred_element_type=jnp.float32)
        tile = (screened[None] * inner).astype(jnp.bfloat16)
        back = jnp.einsum(
            "bmn,nc->bmc", tile, cond_full, preferred_element_type=jnp.float32
        ).astype(jnp.bfloat16)
        part_low = jnp.einsum(
            "mv,bmc->bvc", val_points, back, preferred_element_type=jnp.float32
        ).astype(jnp.bfloat16)
        partial_terms = lax.optimization_barrier(part_low).astype(jnp.float32)
        kernel_full = lax.psum(partial_terms, ("row", "col"))
        x_full = energy_full[None] * x_full + kernel_full
        xb_full = x_full.astype(jnp.bfloat16)
        x_mine = lax.dynamic_slice_in_dim(x_full, offset, width, 2)
    return x_mine


def solution(mesh):
    in_specs = (P(None, None, "row"), P("row", "col"), P("row", None), P("col", "row"), P(), P())
    out_specs = P(None, None, "row")
    return jax.shard_map(body, mesh=mesh, in_specs=in_specs, out_specs=out_specs, check_vma=False)
```

profile of v0, /device:TPU:0, one launch (start us, length us, event | category | flops | bytes accessed | tf_op | source)
XLA Modules:
  0.0 126.8 jit_solution(9335751933009314841)
XLA Ops:
  0.0 0.0 copy-start
  0.0 0.0 copy-start.2
  0.0 11.5 %all_gather.7 = bf16[192,1024]{1,0:T(8,128)(2,1)S(1)} all-gather(bf16[192,128]{1,0:T(8,128)(2,1)} %param.9), channel_id=1, replica_groups=mesh['row'=8,'col'=4] {'row'}, dimensions={1}, use_global_device_ids=true | all-gather | bytes 442368 | tf_op jit(solution)/shard_map/all_gather | solution.py:10
  11.5 0.0 copy-done.2
  11.5 0.1 copy.7
  11.6 0.0 copy-start.1
  11.6 9.6 %all_gather.6 = bf16[1,256,1024]{1,2,0:T(8,128)(2,1)S(1)} all-gather(bf16[1,256,128]{1,2,0:T(8,128)(2,1)S(1)} %copy.7), channel_id=1, replica_groups=mesh['row'=8,'col'=4] {'row'}, dimensions={2}, use_global_device_ids=true | all-gather | bytes 589824 | tf_op jit(solution)/shard_map/all_gather | solution.py:14
  21.2 0.0 copy-done
  21.2 0.0 copy-done.1
  21.2 0.5 fusion.8
  21.7 0.5 fusion
  22.2 0.0 copy-start.3
  22.2 0.0 copy-start.4
  22.3 50.6 %all-reduce.2 = f32[1,256,1024]{1,2,0:T(8,128)S(1)} all-reduce(bf16[1,256,1024]{1,2,0:T(8,128)(2,1)S(1)} %fusion), channel_id=1, replica_groups=mesh['row'=8,'col'=4] {'row','col'}, use_global_device_ids=true, to_apply=%region_0.0 | all-reduce | flops 262144 | bytes 1572864 | tf_op jit(solution)/shard_map/psum | solution.py:32
  72.9 0.0 copy-done.3
  72.9 0.0 copy-done.4
  72.9 1.2 broadcast_subtract_fusion
  74.1 0.5 fusion.9
  74.6 0.5 fusion.1
  75.1 50.0 %all-reduce.3 = f32[1,256,1024]{1,2,0:T(8,128)S(1)} all-reduce(bf16[1,256,1024]{1,2,0:T(8,128)(2,1)S(1)} %fusion.1), channel_id=1, replica_groups=mesh['row'=8,'col'=4] {'row','col'}, use_global_device_ids=true, to_apply=%region_1.0 | all-reduce | flops 262144 | bytes 1572864 | tf_op jit(solution)/shard_map/psum | solution.py:32
  125.1 0.9 dynamic-slice_add_fusion
  126.0 0.8 copy.8
Async XLA Ops:
  0.0 21.2 %copy-start = (bf16[96,256]{1,0:T(8,128)(2,1)S(1)}, bf16[96,256]{1,0:T(8,128)(2,1)}, u32[]{:S(2)}) copy-start(bf16[96,256]{1,0:T(8,128)(2,1)} %param.8) | copy-start | bytes 147460
  0.0 11.5 %copy-start.2 = (f32[1,256,128]{2,1,0:T(8,128)S(1)}, f32[1,256,128]{2,1,0:T(8,128)}, u32[]{:S(2)}) copy-start(f32[1,256,128]{2,1,0:T(8,128)} %param.6) | copy-start | bytes 393220
  11.6 9.6 %copy-start.1 = (bf16[96,192]{1,0:T(8,128)(2,1)S(1)}, bf16[96,192]{1,0:T(8,128)(2,1)}, u32[]{:S(2)}) copy-start(bf16[96,192]{1,0:T(8,128)(2,1)} %param.7) | copy-start | bytes 110596
  22.2 50.6 %copy-start.3 = (f32[1024]{0:T(1024)S(1)}, f32[1024]{0:T(1024)}, u32[]{:S(2)}) copy-start(f32[1024]{0:T(1024)} %param.11) | copy-start | bytes 12292
  22.2 50.6 %copy-start.4 = (f32[256]{0:T(256)S(1)}, f32[256]{0:T(256)}, u32[]{:S(2)}) copy-start(f32[256]{0:T(256)} %param.10) | copy-start | bytes 3076
where the time goes:
time: 127 us
  blocking collectives  122 us (96%)
  other arithmetic  2.13 us (2%)
  matrix products  2.01 us (2%)
    psum x2, blocking collectives, body(): kernel_full = lax.psum(partial_terms, ('row', 'col'))  101 us
    all_gather x1, blocking collectives, body(): cond_full = lax.all_gather(cond_points, 'row', axis=1, tiled=True)  11.5 us
    all_gather x1, blocking collectives, body(): lax.all_gather(trial.astype(jnp.bfloat16), 'row', axis=2, tiled=True)  9.6 us

commit v1 on v0

v1 whole, which is shorter than its diff:
```python
import functools

import jax
import jax.numpy as jnp
from jax import lax
from jax.experimental import pallas as pl
from jax.experimental.pallas import tpu as pltpu
from jax.sharding import PartitionSpec as P

APPLY = 2
LANES = 128
ROWS16 = 16
F32 = jnp.float32
BF16 = jnp.bfloat16
MESH = pl.DeviceIdType.MESH


def dot_nt(a, b):
    return lax.dot_general(a, b, (((1,), (1,)), ((), ())), preferred_element_type=F32)


def dot_tn(a, b):
    return lax.dot_general(a, b, (((0,), (0,)), ((), ())), preferred_element_type=F32)


def kernel(nr, nj, x_ref, s_ref, v_ref, c_ref, ev_ref, ec_ref, out_ref,
           vall, st, sall, asend, arecv, craw, clo, chi, evb,
           ysend0, ysend1, yall0, yall1, esend, erecv, zsend, zrecv, kz0, kz1,
           row_send, row_recv, col_send, col_recv):
    r = lax.axis_index("row")
    j = lax.axis_index("col")
    mb, nv = v_ref.shape
    nb, cw = c_ref.shape
    nk = nb // nr
    slot = st.shape[1]
    half = slot // 2
    vj = nv // nj
    row_peers = [lax.rem(r + k, nr) for k in range(1, nr)]
    col_peers = [lax.rem(j + k, nj) for k in range(1, nj)]

    barrier = pltpu.get_barrier_semaphore()
    for s in row_peers:
        pl.semaphore_signal(barrier, inc=1, device_id=(s, j), device_id_type=MESH)
    for s in col_peers:
        pl.semaphore_signal(barrier, inc=1, device_id=(r, s), device_id_type=MESH)

    def row_copy(phase, src, dst, peer, slot_id):
        return pltpu.make_async_remote_copy(
            src_ref=src, dst_ref=dst, send_sem=row_send.at[phase, peer],
            recv_sem=row_recv.at[phase, slot_id], device_id=(peer, j), device_id_type=MESH)

    def col_copy(phase, src, dst, peer, slot_id):
        return pltpu.make_async_remote_copy(
            src_ref=src, dst_ref=dst, send_sem=col_send.at[phase, peer],
            recv_sem=col_recv.at[phase, slot_id], device_id=(r, peer), device_id_type=MESH)

    pending = []

    def row_start(phase, src_of, dst_of):
        for s in row_peers:
            copy = row_copy(phase, src_of(s), dst_of(r), s, r)
            copy.start()
            pending.append(copy)

    def row_wait(phase, dst_of):
        for s in reversed(row_peers):
            row_copy(phase, dst_of(s), dst_of(s), s, s).wait_recv()

    def col_start(phase, src_of, dst_of):
        for s in col_peers:
            copy = col_copy(phase, src_of(s), dst_of(j), s, j)
            copy.start()
            pending.append(copy)

    def col_wait(phase, dst_of):
        for s in col_peers:
            col_copy(phase, dst_of(s), dst_of(s), s, s).wait_recv()

    pad_rows = jnp.zeros((slot - nk, cw), F32)

    def padded(ref):
        wide = ref[...].astype(F32)
        return [
            jnp.concatenate([wide[i * nk:(i + 1) * nk], pad_rows], axis=0).astype(BF16)
            for i in range(nr)
        ]

    def place(blocks, col):
        for i, block in enumerate(blocks):
            clo[i, col] = block[:half]
            chi[i, col] = block[half:]

    own = padded(c_ref)
    first = dot_nt(jnp.concatenate(own, axis=0), x_ref[0].astype(BF16))
    for i in range(nr):
        asend[i] = first[i * slot:(i + 1) * slot].astype(BF16)
    arecv[r] = asend[r]

    pl.semaphore_wait(barrier, nr - 1 + nj - 1)
    row_start(0, lambda s: asend.at[s], lambda s: arecv.at[s])
    row_start(1, lambda s: v_ref, lambda s: vall.at[s, pl.ds(0, mb)])
    col_start(0, lambda s: c_ref, lambda s: craw.at[s])

    scr = s_ref[...].astype(F32)
    scr = jnp.concatenate([scr, jnp.zeros((LANES - mb, nb), F32)], axis=0)
    wide = -(-nb // LANES) * LANES
    if wide > nb:
        scr = jnp.concatenate([scr, jnp.zeros((LANES, wide - nb), F32)], axis=1)
    scr = scr.T
    for i in range(nr):
        st[i] = jnp.concatenate(
            [scr[i * nk:(i + 1) * nk], jnp.zeros((slot - nk, LANES), F32)], axis=0).astype(BF16)
    row_start(2, lambda s: st.at[s], lambda s: sall.at[s])
    sall[r] = st[r]
    vall[r, pl.ds(0, mb)] = v_ref[...]
    if mb < LANES:
        for i in range(nr):
            vall[i, pl.ds(mb, LANES - mb)] = jnp.zeros((LANES - mb, nv), BF16)
    place(own, j)
    evb[...] = jnp.broadcast_to(ev_ref[...], (LANES, nv)).T
    ec = ec_ref[:, pl.ds(pl.multiple_of(r * cw, cw), cw)]
    low = lax.broadcasted_iota(jnp.int32, (half, LANES), 1) < vj

    def swap(block):
        return pltpu.roll(block, vj, 1)

    def screen(w):
        allv = vall[...].reshape(nr * LANES, nv)
        inner = dot_nt(w, allv)
        tile = jnp.concatenate(
            [(sall[i].astype(F32) * inner[:, i * LANES:(i + 1) * LANES]).astype(BF16)
             for i in range(nr)], axis=1)
        return jnp.dot(tile, allv, preferred_element_type=F32)

    def pack(y, send):
        for p in range(nj // 2):
            top = y[:half, p * LANES:(p + 1) * LANES]
            bottom = y[half:, p * LANES:(p + 1) * LANES]
            send[2 * p] = jnp.where(low, top, swap(bottom)).astype(BF16)
            send[2 * p + 1] = jnp.where(low, swap(top), bottom).astype(BF16)

    def spread(y, send, yall, phase_col, phase_row):
        pack(y, send)
        col_start(phase_col, lambda s: send.at[s], lambda s: yall.at[r, s])
        yall[r, j] = send[j]
        col_wait(phase_col, lambda s: yall.at[r, s])
        row_start(phase_row, lambda s: yall.at[r], lambda s: yall.at[s])

    def term(yall):
        whole = yall[...].reshape(nr * nj * half, LANES)
        lo = clo[...].reshape(nr * nj * half, cw)
        hi = chi[...].reshape(nr * nj * half, cw)
        return dot_tn(whole, lo)[:vj] + dot_tn(whole, hi)[vj:]

    row_wait(0, lambda s: arecv.at[s])
    total = arecv[0].astype(F32)
    for i in range(1, nr):
        total = total + arecv[i].astype(F32)
    w0 = total.astype(BF16)
    row_wait(2, lambda s: sall.at[s])
    row_wait(1, lambda s: vall.at[s, pl.ds(0, mb)])
    spread(screen(w0), ysend0, yall0, 1, 3)
    col_wait(0, lambda s: craw.at[s])
    for s in col_peers:
        place(padded(craw.at[s]), s)
    row_wait(3, lambda s: yall0.at[s])
    k0 = term(yall0)
    mine = pl.ds(pl.multiple_of(j * vj, vj), vj)
    x1 = (ec - evb[mine, :]) * x_ref[0, mine, :] + k0
    x1b = x1.astype(BF16)
    none = jnp.zeros((LANES - vj, cw), BF16)
    lo = clo[...].reshape(nr * nj * half, cw)
    hi = chi[...].reshape(nr * nj * half, cw)
    partial = (dot_nt(lo, jnp.concatenate([x1b, none], axis=0))
               + dot_nt(hi, jnp.concatenate([none, x1b], axis=0)))
    esend[...] = partial.astype(BF16).reshape(esend.shape)
    row_start(4, lambda s: esend.at[s], lambda s: erecv.at[s])
    erecv[r] = esend[r]
    kz0[j] = k0.astype(BF16)
    row_wait(4, lambda s: erecv.at[s])

    total = erecv[0].astype(F32)
    for i in range(1, nr):
        total = total + erecv[i].astype(F32)
    zsend[...] = total.astype(BF16)
    col_start(2, lambda s: zsend.at[s], lambda s: zrecv.at[s])
    col_start(4, lambda s: kz0.at[j], lambda s: kz0.at[s])
    zrecv[j] = zsend[j]
    col_wait(2, lambda s: zrecv.at[s])
    tops, bottoms = [], []
    for p in range(nj // 2):
        a = zrecv[2 * p].astype(F32)
        b = zrecv[2 * p + 1].astype(F32)
        tops.append(jnp.where(low, a, swap(b)))
        bottoms.append(jnp.where(low, swap(a), b))
    w1 = jnp.concatenate(
        [jnp.concatenate(tops, axis=1), jnp.concatenate(bottoms, axis=1)], axis=0).astype(BF16)
    spread(screen(w1), ysend1, yall1, 3, 5)
    col_wait(4, lambda s: kz0.at[s])
    energy = ec - evb[...]
    base = energy * (energy * x_ref[0] + kz0[...].reshape(nv, cw).astype(F32))
    row_wait(5, lambda s: yall1.at[s])
    kz1[j] = term(yall1).astype(BF16)
    col_start(5, lambda s: kz1.at[j], lambda s: kz1.at[s])
    col_wait(5, lambda s: kz1.at[s])
    out_ref[0] = base + kz1[...].reshape(nv, cw).astype(F32)
    for copy in pending:
        copy.wait_send()


def fused(nr, nj, trial, screened, val_points, cond_points, eps_val, eps_cond):
    mb, nv = val_points.shape
    nb, cw = cond_points.shape
    slot = 2 * ROWS16
    half = ROWS16
    scratch = [
        pltpu.VMEM((nr, LANES, nv), BF16),
        pltpu.VMEM((nr, slot, LANES), BF16),
        pltpu.VMEM((nr, slot, LANES), BF16),
        pltpu.VMEM((nr, slot, nv), BF16),
        pltpu.VMEM((nr, slot, nv), BF16),
        pltpu.VMEM((nj, nb, cw), BF16),
        pltpu.VMEM((nr, nj, half, cw), BF16),
        pltpu.VMEM((nr, nj, half, cw), BF16),
        pltpu.VMEM((nv, LANES), F32),
        pltpu.VMEM((nj, half, LANES), BF16),
        pltpu.VMEM((nj, half, LANES), BF16),
        pltpu.VMEM((nr, nj, half, LANES), BF16),
        pltpu.VMEM((nr, nj, half, LANES), BF16),
        pltpu.VMEM((nr, nj, half, LANES), BF16),
        pltpu.VMEM((nr, nj, half, LANES), BF16),
        pltpu.VMEM((nj, half, LANES), BF16),
        pltpu.VMEM((nj, half, LANES), BF16),
        pltpu.VMEM((nj, nv // nj, cw), BF16),
        pltpu.VMEM((nj, nv // nj, cw), BF16),
        pltpu.SemaphoreType.DMA((6, nr)),
        pltpu.SemaphoreType.DMA((6, nr)),
        pltpu.SemaphoreType.DMA((6, nj)),
        pltpu.SemaphoreType.DMA((6, nj)),
    ]
    return pl.pallas_call(
        functools.partial(kernel, nr, nj),
        out_shape=jax.ShapeDtypeStruct(trial.shape, F32),
        in_specs=[pl.BlockSpec(memory_space=pltpu.VMEM)] * 6,
        out_specs=pl.BlockSpec(memory_space=pltpu.VMEM),
        scratch_shapes=scratch,
        compiler_params=pltpu.CompilerParams(
            collective_id=0, has_side_effects=True, vmem_limit_bytes=24 * 2**20),
    )(trial, screened, val_points, cond_points, eps_val[None], eps_cond[None])


def fits(nr, nj, trial, val_points, cond_points):
    mb, nv = val_points.shape
    nb, cw = cond_points.shape
    nk = nb // nr
    return (trial.shape[0] == 1 and cw == LANES and nb % nr == 0 and nk % 8 == 0
            and nk <= 2 * ROWS16 and mb % ROWS16 == 0 and mb <= LANES
            and nj % 2 == 0 and nv % nj == 0 and 2 * (nv // nj) == LANES)


def general(trial, screened, val_points, cond_points, eps_val, eps_cond):
    cond_full = lax.all_gather(cond_points, "row", axis=1, tiled=True)
    energy_full = eps_cond[None, :] - eps_val[:, None]
    width = trial.shape[2]
    offset = lax.axis_index("row") * width
    x_full = lax.all_gather(trial.astype(BF16), "row", axis=2, tiled=True).astype(trial.dtype)
    xb_full = x_full.astype(BF16)
    x_mine = trial
    for step in range(APPLY):
        pair = jnp.einsum(
            "mv,bvc->bmc", val_points, xb_full, preferred_element_type=F32).astype(BF16)
        inner = jnp.einsum("bmc,nc->bmn", pair, cond_full, preferred_element_type=F32)
        tile = (screened[None] * inner).astype(BF16)
        back = jnp.einsum("bmn,nc->bmc", tile, cond_full, preferred_element_type=F32).astype(BF16)
        part_low = jnp.einsum(
            "mv,bmc->bvc", val_points, back, preferred_element_type=F32).astype(BF16)
        partial_terms = lax.optimization_barrier(part_low).astype(F32)
        kernel_full = lax.psum(partial_terms, ("row", "col"))
        x_full = energy_full[None] * x_full + kernel_full
        xb_full = x_full.astype(BF16)
        x_mine = lax.dynamic_slice_in_dim(x_full, offset, width, 2)
    return x_mine


def solution(mesh):
    nr, nj = mesh.shape["row"], mesh.shape["col"]

    def body(trial, screened, val_points, cond_points, eps_val, eps_cond):
        args = (trial, screened, val_points, cond_points, eps_val, eps_cond)
        if fits(nr, nj, trial, val_points, cond_points):
            return fused(nr, nj, *args)
        return general(*args)

    in_specs = (P(None, None, "row"), P("row", "col"), P("row", None), P("col", "row"), P(), P())
    out_specs = P(None, None, "row")
    return jax.shard_map(body, mesh=mesh, in_specs=in_specs, out_specs=out_specs, check_vma=False)
```

time: 127 us -> 47 us (0.37)
  blocking collectives: 122 us -> 0 us
  Pallas kernels: 0 us -> 41.3 us
  local copies, waits for them, and re-layouts: 0.88 us -> 5.32 us
  other arithmetic: 2.13 us -> 0 us
  matrix products: 2.01 us -> 0 us
    psum x2 -> x0, blocking collectives: 101 us -> none  [body(): kernel_full = lax.psum(partial_terms, ('row', 'col'))]
    pallas_call x0 -> x1, Pallas kernels: none -> 41.3 us  [fused(): pl.pallas_call(functools.partial(kernel, nr, nj), out_shape=jax.ShapeDtyp...]
    all_gather x2 -> x0, blocking collectives: 21.1 us -> none  [the longest x1 11.5 us: body(): cond_full = lax.all_gather(cond_points, 'row', axis=1, tiled=True)]
    unnamed x11 -> x13, local copies, waits for them, and re-layouts: 0.12 us -> 5.32 us
    dot_general x4 -> x0, matrix products: 2.01 us -> none  [the longest x2 1.03 us: body(): jnp.einsum('mv,bmc->bvc', val_points, back, preferred_element_type=jnp.fl...]
where the time goes in v1:
time: 47 us; the launch traced here: 46.6 us
  Pallas kernels  41.3 us (88%)
  local copies, waits for them, and re-layouts  5.32 us (11%)
    pallas_call x1, Pallas kernels, fused(): pl.pallas_call(functools.partial(kernel, nr, nj), out_shape=jax.ShapeDtyp...  41.3 us
    unnamed x13, local copies, waits for them, and re-layouts  5.32 us

profile of v1, /device:TPU:0, one launch (start us, length us, event | category | flops | bytes accessed | tf_op | source)
XLA Modules:
  0.0 46.6 jit_solution(5155897082494772131)
XLA Ops:
  0.0 0.0 copy-start.5
  0.0 0.7 %copy-done.5 = f32[256]{0:T(256)S(1)} copy-done((f32[256]{0:T(256)S(1)}, f32[256]{0:T(256)}, u32[]{:S(2)}) %copy-start.5) | copy-done | bytes 1048
  0.7 0.0 copy-start
  0.7 0.9 %copy-done = f32[1,256,128]{2,1,0:T(8,128)S(1)} copy-done((f32[1,256,128]{2,1,0:T(8,128)S(1)}, f32[1,256,128]{2,1,0:T(8,128)}, u32[]{:S(2)}) %copy-start) | copy-done | bytes 131096
  1.6 0.0 copy-start.1
  1.6 0.8 %copy-done.1 = bf16[96,192]{1,0:T(8,128)(2,1)S(1)} copy-done((bf16[96,192]{1,0:T(8,128)(2,1)S(1)}, bf16[96,192]{1,0:T(8,128)(2,1)}, u32[]{:S(2)}) %copy-start.1) | copy-done | bytes 36888
  2.4 0.0 copy-start.2
  2.4 0.8 %copy-done.2 = bf16[96,256]{1,0:T(8,128)(2,1)S(1)} copy-done((bf16[96,256]{1,0:T(8,128)(2,1)S(1)}, bf16[96,256]{1,0:T(8,128)(2,1)}, u32[]{:S(2)}) %copy-start.2) | copy-done | bytes 49176
  3.2 0.0 copy-start.3
  3.2 0.8 %copy-done.3 = bf16[192,128]{1,0:T(8,128)(2,1)S(1)} copy-done((bf16[192,128]{1,0:T(8,128)(2,1)S(1)}, bf16[192,128]{1,0:T(8,128)(2,1)}, u32[]{:S(2)}) %copy-start.3) | copy-done | bytes 49176
  4.0 0.0 copy-start.4
  4.0 0.7 %copy-done.4 = f32[1024]{0:T(1024)S(1)} copy-done((f32[1024]{0:T(1024)S(1)}, f32[1024]{0:T(1024)}, u32[]{:S(2)}) %copy-start.4) | copy-done | bytes 4120
  4.7 41.3 %shard_map.64 = f32[1,256,128]{2,1,0:T(8,128)S(1)} custom-call(f32[1,256,128]{2,1,0:T(8,128)S(1)} %copy-done, bf16[96,192]{1,0:T(8,128)(2,1)S(1)} %copy-done.1, bf16[96,256]{1,0:T(8,128)(2,1)S(1)} %copy-done.2, bf16[192,128]{1,0:T(8,128)(2,1)S(1)} %copy-done.3, f32[1,256]{1,0:T(1,128)S(1)} %bitcast.3, f32[1,1024]{1,0:T(1,128)S(1)} %bitcast.2), custom_call_target="tpu_custom_call" | custom-call | tf_op jit(solution)/shard_map/pallas_call | solution.py:241
  46.0 0.7 %copy.8 = f32[1,256,128]{2,1,0:T(8,128)} copy(f32[1,256,128]{2,1,0:T(8,128)S(1)} %shard_map.64) | data formatting | bytes 262144
Async XLA Ops:
  0.0 0.7 %copy-start.5 = (f32[256]{0:T(256)S(1)}, f32[256]{0:T(256)}, u32[]{:S(2)}) copy-start(f32[256]{0:T(256)} %param.10) | copy-start | bytes 3076
  0.7 0.9 %copy-start = (f32[1,256,128]{2,1,0:T(8,128)S(1)}, f32[1,256,128]{2,1,0:T(8,128)}, u32[]{:S(2)}) copy-start(f32[1,256,128]{2,1,0:T(8,128)} %x_ref.1) | copy-start | bytes 393220
  1.6 0.8 %copy-start.1 = (bf16[96,192]{1,0:T(8,128)(2,1)S(1)}, bf16[96,192]{1,0:T(8,128)(2,1)}, u32[]{:S(2)}) copy-start(bf16[96,192]{1,0:T(8,128)(2,1)} %s_ref.1) | copy-start | bytes 110596
  2.4 0.8 %copy-start.2 = (bf16[96,256]{1,0:T(8,128)(2,1)S(1)}, bf16[96,256]{1,0:T(8,128)(2,1)}, u32[]{:S(2)}) copy-start(bf16[96,256]{1,0:T(8,128)(2,1)} %v_ref.1) | copy-start | bytes 147460
  3.2 0.8 %copy-start.3 = (bf16[192,128]{1,0:T(8,128)(2,1)S(1)}, bf16[192,128]{1,0:T(8,128)(2,1)}, u32[]{:S(2)}) copy-start(bf16[192,128]{1,0:T(8,128)(2,1)} %c_ref.1) | copy-start | bytes 147460
  4.0 0.7 %copy-start.4 = (f32[1024]{0:T(1024)S(1)}, f32[1024]{0:T(1024)}, u32[]{:S(2)}) copy-start(f32[1024]{0:T(1024)} %param.11) | copy-start | bytes 12292

commit v2 on v0

v2 whole, which is shorter than its diff:
```python
import functools

import jax
import jax.numpy as jnp
from jax import lax
from jax.experimental import pallas as pl
from jax.experimental.pallas import tpu as pltpu
from jax.sharding import PartitionSpec as P

APPLY = 2
LANES = 128
ROWS16 = 16
F32 = jnp.float32
BF16 = jnp.bfloat16
MESH = pl.DeviceIdType.MESH


def dot_nt(a, b):
    return lax.dot_general(a, b, (((1,), (1,)), ((), ())), preferred_element_type=F32)


def dot_tn(a, b):
    return lax.dot_general(a, b, (((0,), (0,)), ((), ())), preferred_element_type=F32)


def kernel(nr, nj, x_hbm, s_hbm, v_hbm, c_hbm, ev_hbm, ec_hbm, out_ref,
           xv, sv, cv, evv, ecv, vall, st, sall, asend, arecv, call, evb,
           ysend0, ysend1, yall0, yall1, esend, erecv, kz0,
           local_sem, row_send, row_recv, own_send, own_recv,
           col_send, col_recv, peer_send, peer_recv, mate_send, mate_recv):
    r = lax.axis_index("row")
    j = lax.axis_index("col")
    group, plane = j // 2, lax.rem(j, 2)
    me = r * 2 + plane
    np = nr * 2
    nq = np // nj
    mb, nv = v_hbm.shape
    _, nk, cw = c_hbm.shape
    nb = nq * nk
    vh = nv // 2

    loads = {}
    for i, (name, src, dst) in enumerate([
            ("c", c_hbm, cv), ("x", x_hbm, xv), ("s", s_hbm, sv),
            ("v", v_hbm, vall.at[r, pl.ds(0, mb)]), ("ev", ev_hbm, evv), ("ec", ec_hbm, ecv),
            ("call", c_hbm, call.at[:, j])]):
        loads[name] = pltpu.make_async_copy(src, dst, local_sem.at[i])
        loads[name].start()

    barrier = pltpu.get_barrier_semaphore()
    peers = [lax.rem(me + k, np) for k in range(1, np)]
    row_peers = [lax.rem(r + k, nr) for k in range(1, nr)]
    col_peers = [lax.rem(j + k, nj) for k in range(1, nj)]
    far_groups = [lax.rem(group + k, nj // 2) for k in range(1, nj // 2)]
    for p in peers:
        pl.semaphore_signal(barrier, inc=1, device_id=(p // 2, group * 2 + lax.rem(p, 2)),
                            device_id_type=MESH)
    for g in far_groups:
        for s in range(nr):
            pl.semaphore_signal(barrier, inc=1, device_id=(s, g * 2 + plane),
                                device_id_type=MESH)
        pl.semaphore_signal(barrier, inc=1, device_id=(r, g * 2 + 1 - plane),
                            device_id_type=MESH)
    greeted = np - 1 + (nj // 2 - 1) * (nr + 1)

    pending = []

    def send(copy):
        copy.start()
        pending.append(copy)

    def row_copy(src, dst, peer, slot_id):
        return pltpu.make_async_remote_copy(
            src_ref=src, dst_ref=dst, send_sem=row_send.at[peer],
            recv_sem=row_recv.at[slot_id], device_id=(peer, j), device_id_type=MESH)

    def col_copy(src, dst, peer, slot_id):
        return pltpu.make_async_remote_copy(
            src_ref=src, dst_ref=dst, send_sem=col_send.at[peer],
            recv_sem=col_recv.at[slot_id], device_id=(r, peer), device_id_type=MESH)

    def peer_copy(phase, src, dst, peer, slot_id):
        return pltpu.make_async_remote_copy(
            src_ref=src, dst_ref=dst, send_sem=peer_send.at[phase, peer],
            recv_sem=peer_recv.at[phase, slot_id],
            device_id=(peer // 2, group * 2 + lax.rem(peer, 2)), device_id_type=MESH)

    def owner_copy(phase, src, dst, q, g):
        return pltpu.make_async_remote_copy(
            src_ref=src, dst_ref=dst, send_sem=own_send.at[phase, q, g],
            recv_sem=own_recv.at[phase, r],
            device_id=(q * (nj // 2) + group, g * 2 + plane), device_id_type=MESH)

    def is_self(q, g):
        return jnp.logical_and(q * (nj // 2) + group == r, group == g)

    def owner_send(phase, buffer, target):
        for g in range(nj // 2):
            for q in range(nq):
                @pl.when(jnp.logical_not(is_self(q, g)))
                def _():
                    owner_copy(phase, buffer.at[q], target.at[r], q, g).start()

                @pl.when(is_self(q, g))
                def _():
                    target[r] = buffer[q]

    def owner_wait_send(phase, buffer, target):
        for g in range(nj // 2):
            for q in range(nq):
                @pl.when(jnp.logical_not(is_self(q, g)))
                def _():
                    owner_copy(phase, buffer.at[q], target.at[r], q, g).wait_send()

    holder = lax.rem(r, nj // 2) * 2 + plane

    def owner_wait(phase, target):
        for k in range(nr):
            s = lax.rem(r + k, nr)

            def wait():
                pltpu.make_async_remote_copy(
                    src_ref=target.at[s], dst_ref=target.at[s], send_sem=own_send.at[phase, 0, 0],
                    recv_sem=own_recv.at[phase, s], device_id=(s, holder),
                    device_id_type=MESH).wait_recv()

            if k == 0:
                pl.when(holder != j)(wait)
            else:
                wait()

    def all_send(phase, src_of, dst):
        for p in peers:
            send(peer_copy(phase, src_of(p), dst, p, me))

    def all_wait(phase, dst_of):
        for p in reversed(peers):
            peer_copy(phase, dst_of(p), dst_of(p), p, p).wait_recv()

    loads["c"].wait()
    loads["x"].wait()
    first = dot_nt(cv[...].reshape(nb, cw), xv[0].astype(BF16))
    asend[...] = first.astype(BF16).reshape(asend.shape)

    pl.semaphore_wait(barrier, greeted)
    owner_send(0, asend, arecv)
    for s in row_peers:
        send(row_copy(v_hbm, vall.at[r, pl.ds(0, mb)], s, r))

    loads["s"].wait()
    scr = sv[...].astype(F32)
    scr = jnp.concatenate([scr, jnp.zeros((LANES - mb, nb), F32)], axis=0)
    wide = -(-nb // LANES) * LANES
    if wide > nb:
        scr = jnp.concatenate([scr, jnp.zeros((LANES, wide - nb), F32)], axis=1)
    scr = scr.T
    st[...] = scr[:nb].astype(BF16).reshape(st.shape)
    owner_send(1, st, sall)
    for s in col_peers:
        send(col_copy(c_hbm, call.at[:, j], s, j))

    if mb < LANES:
        for i in range(nr):
            vall[i, pl.ds(mb, LANES - mb)] = jnp.zeros((LANES - mb, nv), BF16)
    for name in ("ev", "ec", "v", "call"):
        loads[name].wait()
    evb[...] = jnp.broadcast_to(evv[...], (LANES, nv)).T
    ec = ecv[:, pl.ds(pl.multiple_of(r * cw, cw), cw)]

    def screen(w):
        allv = vall[...].reshape(nr * LANES, nv)
        inner = dot_nt(w, allv)
        tile = jnp.concatenate(
            [(sall[i].astype(F32) * inner[:, i * LANES:(i + 1) * LANES]).astype(BF16)
             for i in range(nr)], axis=1)
        return jnp.dot(tile, allv, preferred_element_type=F32).astype(BF16)

    owner_wait(0, arecv)
    total = arecv[0].astype(F32)
    for i in range(1, nr):
        total = total + arecv[i].astype(F32)
    w0 = total.astype(BF16)
    for s in reversed(row_peers):
        block = vall.at[s, pl.ds(0, mb)]
        row_copy(block, block, s, s).wait_recv()
    owner_wait(1, sall)
    y0 = screen(w0)
    ysend0[0] = y0[:, :vh]
    ysend0[1] = y0[:, vh:]
    all_send(0, lambda p: ysend0.at[lax.rem(p, 2)], yall0.at[me])
    yall0[me] = ysend0[plane]
    for s in col_peers:
        block = call.at[:, s]
        col_copy(block, block, s, s).wait_recv()
    all_wait(0, lambda p: yall0.at[p])
    cond = call[...].reshape(np * nk, cw)
    k0 = dot_tn(yall0[...].reshape(np * nk, vh), cond)
    mine = pl.ds(pl.multiple_of(plane * vh, vh), vh)
    x1 = (ec - evb[mine, :]) * xv[0, mine, :] + k0
    esend[...] = dot_nt(cond, x1.astype(BF16)).astype(BF16).reshape(esend.shape)
    all_send(1, lambda p: esend.at[p], erecv.at[plane, r])
    erecv[plane, r] = esend[me]
    kz0[plane] = k0.astype(BF16)

    def mate_copy(which):
        return pltpu.make_async_remote_copy(
            src_ref=kz0.at[which], dst_ref=kz0.at[which], send_sem=mate_send.at[0],
            recv_sem=mate_recv.at[0], device_id=(r, group * 2 + 1 - plane), device_id_type=MESH)

    send(mate_copy(plane))
    all_wait(1, lambda p: erecv.at[lax.rem(p, 2), p // 2])

    halves = []
    for h in range(2):
        total = erecv[h, 0].astype(F32)
        for i in range(1, nr):
            total = total + erecv[h, i].astype(F32)
        halves.append(total)
    y1 = screen(jnp.concatenate(halves, axis=1).astype(BF16))
    ysend1[...] = y1
    all_send(2, lambda p: ysend1, yall1.at[me])
    yall1[me] = ysend1[...]
    mate_copy(1 - plane).wait_recv()
    energy = ec - evb[...]
    base = energy * (energy * xv[0] + kz0[...].reshape(nv, cw).astype(F32))
    all_wait(2, lambda p: yall1.at[p])
    out_ref[0] = base + dot_tn(yall1[...].reshape(np * nk, nv), cond)
    for copy in pending:
        copy.wait_send()
    owner_wait_send(0, asend, arecv)
    owner_wait_send(1, st, sall)


def fused(nr, nj, trial, screened, val_points, cond_points, eps_val, eps_cond):
    mb, nv = val_points.shape
    nb, cw = cond_points.shape
    np = 2 * nr
    nq = np // nj
    nk = nb // nq
    vh = nv // 2
    ng = nj // 2
    scratch = [
        pltpu.VMEM(trial.shape, F32),
        pltpu.VMEM(screened.shape, BF16),
        pltpu.VMEM((nq, nk, cw), BF16),
        pltpu.VMEM((1, nv), F32),
        pltpu.VMEM((1, eps_cond.shape[0]), F32),
        pltpu.VMEM((nr, LANES, nv), BF16),
        pltpu.VMEM((nq, nk, LANES), BF16),
        pltpu.VMEM((nr, nk, LANES), BF16),
        pltpu.VMEM((nq, nk, nv), BF16),
        pltpu.VMEM((nr, nk, nv), BF16),
        pltpu.VMEM((nq, nj, nk, cw), BF16),
        pltpu.VMEM((nv, LANES), F32),
        pltpu.VMEM((2, nk, vh), BF16),
        pltpu.VMEM((nk, nv), BF16),
        pltpu.VMEM((np, nk, vh), BF16),
        pltpu.VMEM((np, nk, nv), BF16),
        pltpu.VMEM((np, nk, vh), BF16),
        pltpu.VMEM((2, nr, nk, vh), BF16),
        pltpu.VMEM((2, vh, cw), BF16),
        pltpu.SemaphoreType.DMA((7,)),
        pltpu.SemaphoreType.DMA((nr,)),
        pltpu.SemaphoreType.DMA((nr,)),
        pltpu.SemaphoreType.DMA((2, nq, ng)),
        pltpu.SemaphoreType.DMA((2, nr)),
        pltpu.SemaphoreType.DMA((nj,)),
        pltpu.SemaphoreType.DMA((nj,)),
        pltpu.SemaphoreType.DMA((3, np)),
        pltpu.SemaphoreType.DMA((3, np)),
        pltpu.SemaphoreType.DMA((1,)),
        pltpu.SemaphoreType.DMA((1,)),
    ]
    return pl.pallas_call(
        functools.partial(kernel, nr, nj),
        out_shape=jax.ShapeDtypeStruct(trial.shape, F32),
        in_specs=[pl.BlockSpec(memory_space=pl.ANY)] * 6,
        out_specs=pl.BlockSpec(memory_space=pltpu.VMEM),
        scratch_shapes=scratch,
        compiler_params=pltpu.CompilerParams(
            collective_id=0, has_side_effects=True, vmem_limit_bytes=48 * 2**20),
    )(trial, screened, val_points, cond_points.reshape(nq, nk, cw), eps_val[None], eps_cond[None])


def fits(nr, nj, trial, val_points, cond_points):
    mb, nv = val_points.shape
    nb, cw = cond_points.shape
    if nj % 2 or (2 * nr) % nj or nb % (2 * nr // nj):
        return False
    nk = nb // (2 * nr // nj)
    return (trial.shape[0] == 1 and cw == LANES and nk % ROWS16 == 0
            and mb % ROWS16 == 0 and mb <= LANES and nv == 2 * LANES)


def general(trial, screened, val_points, cond_points, eps_val, eps_cond):
    cond_full = lax.all_gather(cond_points, "row", axis=1, tiled=True)
    energy_full = eps_cond[None, :] - eps_val[:, None]
    width = trial.shape[2]
    offset = lax.axis_index("row") * width
    x_full = lax.all_gather(trial.astype(BF16), "row", axis=2, tiled=True).astype(trial.dtype)
    xb_full = x_full.astype(BF16)
    x_mine = trial
    for step in range(APPLY):
        pair = jnp.einsum(
            "mv,bvc->bmc", val_points, xb_full, preferred_element_type=F32).astype(BF16)
        inner = jnp.einsum("bmc,nc->bmn", pair, cond_full, preferred_element_type=F32)
        tile = (screened[None] * inner).astype(BF16)
        back = jnp.einsum("bmn,nc->bmc", tile, cond_full, preferred_element_type=F32).astype(BF16)
        part_low = jnp.einsum(
            "mv,bmc->bvc", val_points, back, preferred_element_type=F32).astype(BF16)
        partial_terms = lax.optimization_barrier(part_low).astype(F32)
        kernel_full = lax.psum(partial_terms, ("row", "col"))
        x_full = energy_full[None] * x_full + kernel_full
        xb_full = x_full.astype(BF16)
        x_mine = lax.dynamic_slice_in_dim(x_full, offset, width, 2)
    return x_mine


def solution(mesh):
    nr, nj = mesh.shape["row"], mesh.shape["col"]

    def body(trial, screened, val_points, cond_points, eps_val, eps_cond):
        args = (trial, screened, val_points, cond_points, eps_val, eps_cond)
        if fits(nr, nj, trial, val_points, cond_points):
            return fused(nr, nj, *args)
        return general(*args)

    in_specs = (P(None, None, "row"), P("row", "col"), P("row", None), P("col", "row"), P(), P())
    out_specs = P(None, None, "row")
    return jax.shard_map(body, mesh=mesh, in_specs=in_specs, out_specs=out_specs, check_vma=False)
```

time: 127 us -> 40.4 us (0.32)
  blocking collectives: 122 us -> 0 us
  Pallas kernels: 0 us -> 35.4 us
  local copies, waits for them, and re-layouts: 0.88 us -> 4.65 us
  other arithmetic: 2.13 us -> 0 us
  matrix products: 2.01 us -> 0 us
    psum x2 -> x0, blocking collectives: 101 us -> none  [body(): kernel_full = lax.psum(partial_terms, ('row', 'col'))]
    pallas_call x0 -> x1, Pallas kernels: none -> 35.4 us  [fused(): pl.pallas_call(functools.partial(kernel, nr, nj), out_shape=jax.ShapeDtyp...]
    all_gather x2 -> x0, blocking collectives: 21.1 us -> none  [the longest x1 11.5 us: body(): cond_full = lax.all_gather(cond_points, 'row', axis=1, tiled=True)]
    unnamed x11 -> x13, local copies, waits for them, and re-layouts: 0.12 us -> 4.65 us
    dot_general x4 -> x0, matrix products: 2.01 us -> none  [the longest x2 1.03 us: body(): jnp.einsum('mv,bmc->bvc', val_points, back, preferred_element_type=jnp.fl...]
where the time goes in v2:
time: 40.4 us; the launch traced here: 40.1 us
  Pallas kernels  35.4 us (88%)
  local copies, waits for them, and re-layouts  4.65 us (12%)
    pallas_call x1, Pallas kernels, fused(): pl.pallas_call(functools.partial(kernel, nr, nj), out_shape=jax.ShapeDtyp...  35.4 us
    unnamed x13, local copies, waits for them, and re-layouts  4.65 us

profile of v2, /device:TPU:0, one launch (start us, length us, event | category | flops | bytes accessed | tf_op | source)
XLA Modules:
  0.0 40.1 jit_solution(6510784099026788997)
XLA Ops:
  0.0 0.0 copy-start.4
  0.0 0.0 copy-start.5
  0.0 0.7 %copy-done.4 = f32[1024]{0:T(1024)S(1)} copy-done((f32[1024]{0:T(1024)S(1)}, f32[1024]{0:T(1024)}, u32[]{:S(2)}) %copy-start.4) | copy-done | bytes 4120
  0.7 0.0 copy-done.5
  0.7 0.0 copy-start
  0.7 0.9 %copy-done = f32[1,256,128]{2,1,0:T(8,128)S(1)} copy-done((f32[1,256,128]{2,1,0:T(8,128)S(1)}, f32[1,256,128]{2,1,0:T(8,128)}, u32[]{:S(2)}) %copy-start) | copy-done | bytes 131096
  1.6 0.0 copy-start.1
  1.6 0.8 %copy-done.1 = bf16[96,192]{1,0:T(8,128)(2,1)S(1)} copy-done((bf16[96,192]{1,0:T(8,128)(2,1)S(1)}, bf16[96,192]{1,0:T(8,128)(2,1)}, u32[]{:S(2)}) %copy-start.1) | copy-done | bytes 36888
  2.4 0.0 copy-start.2
  2.4 0.8 %copy-done.2 = bf16[96,256]{1,0:T(8,128)(2,1)S(1)} copy-done((bf16[96,256]{1,0:T(8,128)(2,1)S(1)}, bf16[96,256]{1,0:T(8,128)(2,1)}, u32[]{:S(2)}) %copy-start.2) | copy-done | bytes 49176
  3.2 0.0 copy-start.3
  3.2 0.8 %copy-done.3 = bf16[192,128]{1,0:T(8,128)(2,1)S(1)} copy-done((bf16[192,128]{1,0:T(8,128)(2,1)S(1)}, bf16[192,128]{1,0:T(8,128)(2,1)}, u32[]{:S(2)}) %copy-start.3) | copy-done | bytes 49176
  4.0 35.4 %shard_map.64 = f32[1,256,128]{2,1,0:T(8,128)S(1)} custom-call(f32[1,256,128]{2,1,0:T(8,128)S(1)} %copy-done, bf16[96,192]{1,0:T(8,128)(2,1)S(1)} %copy-done.1, bf16[96,256]{1,0:T(8,128)(2,1)S(1)} %copy-done.2, bf16[4,48,128]{2,1,0:T(8,128)(2,1)S(1)} %bitcast.3, f32[1,256]{1,0:T(1,128)S(1)} %bitcast.5, f32[1,1024]{1,0:T(1,128)S(1)} %bitcast.4), custom_call_target="tpu_custom_call" | custom-call | tf_op jit(solution)/shard_map/pallas_call | solution.py:274
  39.5 0.7 %copy.8 = f32[1,256,128]{2,1,0:T(8,128)} copy(f32[1,256,128]{2,1,0:T(8,128)S(1)} %shard_map.64) | data formatting | bytes 262144
Async XLA Ops:
  0.0 0.7 %copy-start.4 = (f32[1024]{0:T(1024)S(1)}, f32[1024]{0:T(1024)}, u32[]{:S(2)}) copy-start(f32[1024]{0:T(1024)} %param.11) | copy-start | bytes 12292
  0.0 0.7 %copy-start.5 = (f32[256]{0:T(256)S(1)}, f32[256]{0:T(256)}, u32[]{:S(2)}) copy-start(f32[256]{0:T(256)} %param.10) | copy-start | bytes 3076
  0.7 0.9 %copy-start = (f32[1,256,128]{2,1,0:T(8,128)S(1)}, f32[1,256,128]{2,1,0:T(8,128)}, u32[]{:S(2)}) copy-start(f32[1,256,128]{2,1,0:T(8,128)} %x_hbm.1) | copy-start | bytes 393220
  1.6 0.8 %copy-start.1 = (bf16[96,192]{1,0:T(8,128)(2,1)S(1)}, bf16[96,192]{1,0:T(8,128)(2,1)}, u32[]{:S(2)}) copy-start(bf16[96,192]{1,0:T(8,128)(2,1)} %s_hbm.1) | copy-start | bytes 110596
  2.4 0.8 %copy-start.2 = (bf16[96,256]{1,0:T(8,128)(2,1)S(1)}, bf16[96,256]{1,0:T(8,128)(2,1)}, u32[]{:S(2)}) copy-start(bf16[96,256]{1,0:T(8,128)(2,1)} %v_hbm.1) | copy-start | bytes 147460
  3.2 0.8 %copy-start.3 = (bf16[192,128]{1,0:T(8,128)(2,1)S(1)}, bf16[192,128]{1,0:T(8,128)(2,1)}, u32[]{:S(2)}) copy-start(bf16[192,128]{1,0:T(8,128)(2,1)} %param.9) | copy-start | bytes 147460

commit v3 on v2

--- a/solution.py
+++ b/solution.py
@@ -19,15 +19,11 @@
     return lax.dot_general(a, b, (((1,), (1,)), ((), ())), preferred_element_type=F32)
 
 
-def dot_tn(a, b):
-    return lax.dot_general(a, b, (((0,), (0,)), ((), ())), preferred_element_type=F32)
-
-
 def kernel(nr, nj, x_hbm, s_hbm, v_hbm, c_hbm, ev_hbm, ec_hbm, out_ref,
            xv, sv, cv, evv, ecv, vall, st, sall, asend, arecv, call, evb,
-           ysend0, ysend1, yall0, yall1, esend, erecv, kz0,
+           ysend0, ysend1, yall0, yall1, esend, erecv, kz0, w0, b1t, condt,
            local_sem, row_send, row_recv, own_send, own_recv,
-           col_send, col_recv, peer_send, peer_recv, mate_send, mate_recv):
+           col_send, col_recv, peer_send, peer_recv, mate_send, mate_recv, far_send, far_recv):
     r = lax.axis_index("row")
     j = lax.axis_index("col")
     group, plane = j // 2, lax.rem(j, 2)
@@ -48,7 +44,9 @@
         loads[name].start()
 
     barrier = pltpu.get_barrier_semaphore()
-    peers = [lax.rem(me + k, np) for k in range(1, np)]
+    steps = sorted(range(1, np), key=lambda k: abs(k - np // 2))
+    peers = [lax.rem(me + k, np) for k in steps]
+    sources = [lax.rem(me + np - k, np) for k in steps]
     row_peers = [lax.rem(r + k, nr) for k in range(1, nr)]
     col_peers = [lax.rem(j + k, nj) for k in range(1, nj)]
     far_groups = [lax.rem(group + k, nj // 2) for k in range(1, nj // 2)]
@@ -94,58 +92,62 @@
     def is_self(q, g):
         return jnp.logical_and(q * (nj // 2) + group == r, group == g)
 
-    def owner_send(phase, buffer, target):
-        for g in range(nj // 2):
+    groups = [lax.rem(group + k, nj // 2) for k in range(nj // 2)]
+
+    def owner_each(q, g, away, here):
+        if g is groups[0]:
+            itself = q * (nj // 2) + group == r
+            pl.when(jnp.logical_not(itself))(away)
+            if here is not None:
+                pl.when(itself)(here)
+        else:
+            away()
+
+    def owner_send(phase, buffer, target, chosen):
+        for g in chosen:
             for q in range(nq):
-                @pl.when(jnp.logical_not(is_self(q, g)))
-                def _():
+                def away():
                     owner_copy(phase, buffer.at[q], target.at[r], q, g).start()
 
-                @pl.when(is_self(q, g))
-                def _():
+                def here():
                     target[r] = buffer[q]
 
-    def owner_wait_send(phase, buffer, target):
-        for g in range(nj // 2):
+                owner_each(q, g, away, here)
+
+    def owner_wait_send(phase, buffer, target, chosen):
+        for g in chosen:
             for q in range(nq):
-                @pl.when(jnp.logical_not(is_self(q, g)))
-                def _():
+                def away():
                     owner_copy(phase, buffer.at[q], target.at[r], q, g).wait_send()
 
+                owner_each(q, g, away, None)
+
     holder = lax.rem(r, nj // 2) * 2 + plane
-
-    def owner_wait(phase, target):
-        for k in range(nr):
-            s = lax.rem(r + k, nr)
-
-            def wait():
-                pltpu.make_async_remote_copy(
-                    src_ref=target.at[s], dst_ref=target.at[s], send_sem=own_send.at[phase, 0, 0],
-                    recv_sem=own_recv.at[phase, s], device_id=(s, holder),
-                    device_id_type=MESH).wait_recv()
-
-            if k == 0:
-                pl.when(holder != j)(wait)
-            else:
-                wait()
+    holds = holder == j
+
+    def owner_wait(phase, target, s):
+        pltpu.make_async_remote_copy(
+            src_ref=target.at[s], dst_ref=target.at[s], send_sem=own_send.at[phase, 0, 0],
+            recv_sem=own_recv.at[phase, s], device_id=(s, holder),
+            device_id_type=MESH).wait_recv()
+
+    def far_copy(g):
+        return pltpu.make_async_remote_copy(
+            src_ref=w0, dst_ref=w0, send_sem=far_send.at[g], recv_sem=far_recv.at[0],
+            device_id=(r, g * 2 + plane), device_id_type=MESH)
 
     def all_send(phase, src_of, dst):
         for p in peers:
             send(peer_copy(phase, src_of(p), dst, p, me))
 
     def all_wait(phase, dst_of):
-        for p in reversed(peers):
+        for p in sources:
             peer_copy(phase, dst_of(p), dst_of(p), p, p).wait_recv()
 
     loads["c"].wait()
     loads["x"].wait()
     first = dot_nt(cv[...].reshape(nb, cw), xv[0].astype(BF16))
     asend[...] = first.astype(BF16).reshape(asend.shape)
-
-    pl.semaphore_wait(barrier, greeted)
-    owner_send(0, asend, arecv)
-    for s in row_peers:
-        send(row_copy(v_hbm, vall.at[r, pl.ds(0, mb)], s, r))
 
     loads["s"].wait()
     scr = sv[...].astype(F32)
@@ -155,7 +157,13 @@
         scr = jnp.concatenate([scr, jnp.zeros((LANES, wide - nb), F32)], axis=1)
     scr = scr.T
     st[...] = scr[:nb].astype(BF16).reshape(st.shape)
-    owner_send(1, st, sall)
+
+    pl.semaphore_wait(barrier, greeted)
+    owner_send(0, asend, arecv, groups[:1])
+    owner_send(1, st, sall, groups[1:])
+    for s in row_peers:
+        send(row_copy(v_hbm, vall.at[r, pl.ds(0, mb)], s, r))
+    owner_send(1, st, sall, groups[:1])
     for s in col_peers:
         send(col_copy(c_hbm, call.at[:, j], s, j))
 
@@ -175,16 +183,32 @@
              for i in range(nr)], axis=1)
         return jnp.dot(tile, allv, preferred_element_type=F32).astype(BF16)
 
-    owner_wait(0, arecv)
-    total = arecv[0].astype(F32)
-    for i in range(1, nr):
-        total = total + arecv[i].astype(F32)
-    w0 = total.astype(BF16)
+    mine = pl.ds(pl.multiple_of(plane * vh, vh), vh)
+    b1t[...] = ((ec - evb[mine, :]) * xv[0, mine, :]).T
+
+    @pl.when(holds)
+    def _():
+        for k in range(1, nr):
+            owner_wait(0, arecv, lax.rem(r + k, nr))
+        total = arecv[0].astype(F32)
+        for i in range(1, nr):
+            total = total + arecv[i].astype(F32)
+        w0[...] = total.astype(BF16)
+        for g in groups[1:]:
+            far_copy(g).start()
+
     for s in reversed(row_peers):
         block = vall.at[s, pl.ds(0, mb)]
         row_copy(block, block, s, s).wait_recv()
-    owner_wait(1, sall)
-    y0 = screen(w0)
+    for k in range(1, nr):
+        owner_wait(1, sall, lax.rem(r + k, nr))
+
+    @pl.when(jnp.logical_not(holds))
+    def _():
+        owner_wait(1, sall, r)
+        far_copy(group).wait_recv()
+
+    y0 = screen(w0[...])
     ysend0[0] = y0[:, :vh]
     ysend0[1] = y0[:, vh:]
     all_send(0, lambda p: ysend0.at[lax.rem(p, 2)], yall0.at[me])
@@ -192,15 +216,21 @@
     for s in col_peers:
         block = call.at[:, s]
         col_copy(block, block, s, s).wait_recv()
+    condt[...] = call[...].reshape(np * nk, cw).T
     all_wait(0, lambda p: yall0.at[p])
-    cond = call[...].reshape(np * nk, cw)
-    k0 = dot_tn(yall0[...].reshape(np * nk, vh), cond)
-    mine = pl.ds(pl.multiple_of(plane * vh, vh), vh)
-    x1 = (ec - evb[mine, :]) * xv[0, mine, :] + k0
-    esend[...] = dot_nt(cond, x1.astype(BF16)).astype(BF16).reshape(esend.shape)
-    all_send(1, lambda p: esend.at[p], erecv.at[plane, r])
+    k0t = jnp.dot(condt[...], yall0[...].reshape(np * nk, vh), preferred_element_type=F32)
+    x1t = (b1t[...] + k0t).astype(BF16)
+
+    def kernel_block(p):
+        cond = call[p // nj, lax.rem(p, nj)]
+        esend[p] = jnp.dot(cond, x1t, preferred_element_type=F32).astype(BF16)
+
+    for p in peers:
+        kernel_block(p)
+        send(peer_copy(1, esend.at[p], erecv.at[plane, r], p, me))
+    kernel_block(me)
     erecv[plane, r] = esend[me]
-    kz0[plane] = k0.astype(BF16)
+    kz0[plane] = k0t.astype(BF16)
 
     def mate_copy(which):
         return pltpu.make_async_remote_copy(
@@ -216,19 +246,25 @@
         for i in range(1, nr):
             total = total + erecv[h, i].astype(F32)
         halves.append(total)
-    y1 = screen(jnp.concatenate(halves, axis=1).astype(BF16))
-    ysend1[...] = y1
+    ysend1[...] = screen(jnp.concatenate(halves, axis=1).astype(BF16))
     all_send(2, lambda p: ysend1, yall1.at[me])
     yall1[me] = ysend1[...]
     mate_copy(1 - plane).wait_recv()
     energy = ec - evb[...]
-    base = energy * (energy * xv[0] + kz0[...].reshape(nv, cw).astype(F32))
+    k0 = jnp.concatenate([kz0[h].astype(F32).T for h in range(2)], axis=0)
+    out_ref[0] = energy * (energy * xv[0] + k0)
     all_wait(2, lambda p: yall1.at[p])
-    out_ref[0] = base + dot_tn(yall1[...].reshape(np * nk, nv), cond)
+    k1t = jnp.dot(condt[...], yall1[...].reshape(np * nk, nv), preferred_element_type=F32)
+    out_ref[0] += k1t.T
     for copy in pending:
         copy.wait_send()
-    owner_wait_send(0, asend, arecv)
-    owner_wait_send(1, st, sall)
+    owner_wait_send(0, asend, arecv, groups[:1])
+    owner_wait_send(1, st, sall, groups)
+
+    @pl.when(holds)
+    def _():
+        for g in groups[1:]:
+            far_copy(g).wait_send()
 
 
 def fused(nr, nj, trial, screened, val_points, cond_points, eps_val, eps_cond):
@@ -258,7 +294,10 @@
         pltpu.VMEM((np, nk, nv), BF16),
         pltpu.VMEM((np, nk, vh), BF16),
         pltpu.VMEM((2, nr, nk, vh), BF16),
-        pltpu.VMEM((2, vh, cw), BF16),
+        pltpu.VMEM((2, cw, vh), BF16),
+        pltpu.VMEM((nk, nv), BF16),
+        pltpu.VMEM((cw, vh), F32),
+        pltpu.VMEM((cw, np * nk), BF16),
         pltpu.SemaphoreType.DMA((7,)),
         pltpu.SemaphoreType.DMA((nr,)),
         pltpu.SemaphoreType.DMA((nr,)),
@@ -270,15 +309,17 @@
         pltpu.SemaphoreType.DMA((3, np)),
         pltpu.SemaphoreType.DMA((1,)),
         pltpu.SemaphoreType.DMA((1,)),
+        pltpu.SemaphoreType.DMA((ng,)),
+        pltpu.SemaphoreType.DMA((1,)),
     ]
     return pl.pallas_call(
         functools.partial(kernel, nr, nj),
         out_shape=jax.ShapeDtypeStruct(trial.shape, F32),
-        in_specs=[pl.BlockSpec(memory_space=pl.ANY)] * 6,
+        in_specs=[pl.BlockSpec(memory_space=pltpu.HBM)] * 6,
         out_specs=pl.BlockSpec(memory_space=pltpu.VMEM),
         scratch_shapes=scratch,
         compiler_params=pltpu.CompilerParams(
-            collective_id=0, has_side_effects=True, vmem_limit_bytes=48 * 2**20),
+            collective_id=0, has_side_effects=True, vmem_limit_bytes=64 * 2**20 - 65536),
     )(trial, screened, val_points, cond_points.reshape(nq, nk, cw), eps_val[None], eps_cond[None])
 
 

time: 40.4 us -> 36.3 us (0.90)
  local copies, waits for them, and re-layouts: 4.65 us -> 1.57 us
  Pallas kernels: 35.4 us -> 34.6 us
    unnamed x13 -> x1, local copies, waits for them, and re-layouts: 4.65 us -> 1.57 us
    pallas_call x1, Pallas kernels: 35.4 us -> 34.6 us  [fused(): pl.pallas_call(functools.partial(kernel, nr, nj), out_shape=jax.ShapeDtyp...]
where the time goes in v3:
time: 36.3 us; the launch traced here: 36.1 us
  Pallas kernels  34.6 us (95%)
  local copies, waits for them, and re-layouts  1.57 us (4%)
    pallas_call x1, Pallas kernels, fused(): pl.pallas_call(functools.partial(kernel, nr, nj), out_shape=jax.ShapeDtyp...  34.6 us
    unnamed x1, local copies, waits for them, and re-layouts  1.57 us

profile of v3, /device:TPU:0, one launch (start us, length us, event | category | flops | bytes accessed | tf_op | source)
XLA Modules:
  0.0 36.1 jit_solution(3551086560772627082)
XLA Ops:
  0.0 34.6 %shard_map.64 = f32[1,256,128]{2,1,0:T(8,128)} custom-call(f32[1,256,128]{2,1,0:T(8,128)} %x_hbm.1, bf16[96,192]{1,0:T(8,128)(2,1)} %s_hbm.1, bf16[96,256]{1,0:T(8,128)(2,1)} %v_hbm.1, bf16[4,48,128]{2,1,0:T(8,128)(2,1)} %bitcast.3, f32[1,256]{1,0:T(1,128)} %bitcast.5, f32[1,1024]{1,0:T(1,128)} %bitcast.4), custom_call_target="tpu_custom_call" | custom-call | tf_op jit(solution)/shard_map/pallas_call | solution.py:315
  34.6 1.6 %copy.8 = f32[1,256,128]{2,1,0:T(8,128)} copy(f32[1,256,128]{2,1,0:T(8,128)} %shard_map.64) | data formatting | bytes 262144

commit v4 on v3

v4 whole, which is shorter than its diff:
```python
import functools

import jax
import jax.numpy as jnp
from jax import lax
from jax.experimental import pallas as pl
from jax.experimental.pallas import tpu as pltpu
from jax.sharding import PartitionSpec as P

APPLY = 2
LANES = 128
ROWS16 = 16
F32 = jnp.float32
BF16 = jnp.bfloat16
MESH = pl.DeviceIdType.MESH


def dot_nt(a, b):
    return lax.dot_general(a, b, (((1,), (1,)), ((), ())), preferred_element_type=F32)


def kernel(nr, nj, x_hbm, s_hbm, v_hbm, c_hbm, ev_hbm, ec_hbm, base_hbm, k1_ref,
           xv, sv, cv, evv, ecv, vall, st, sall, asend, arecv, call, evb,
           ysend0, ysend1, yall0, yall1, esend, erecv, kz0, w0, b1t, condt, basev,
           local_sem, own_send, own_recv, col_send, col_recv, peer_send, peer_recv,
           mate_send, mate_recv, far_send, far_recv,
           val_send, val_recv, pass_send, pass_recv):
    r = lax.axis_index("row")
    j = lax.axis_index("col")
    group, plane = j // 2, lax.rem(j, 2)
    me = r * 2 + plane
    np = nr * 2
    nq = np // nj
    mb, nv = v_hbm.shape
    _, nk, cw = c_hbm.shape
    nb = nq * nk
    vh = nv // 2

    loads = {}

    def load(names):
        for name, src, dst in names:
            loads[name] = pltpu.make_async_copy(src, dst, local_sem.at[len(loads)])
            loads[name].start()

    load([("c", c_hbm, cv), ("x", x_hbm, xv)])
    barrier = pltpu.get_barrier_semaphore()
    steps = sorted(range(1, np), key=lambda k: abs(k - np // 2))
    peers = [lax.rem(me + k, np) for k in steps]
    chips = [lax.rem(r + 2 * k, nr) for k in range(1, nr // 2)]
    mate = r + 1 - 2 * lax.rem(r, 2)
    col_peers = [lax.rem(j + k, nj) for k in range(1, nj)]
    far_groups = [lax.rem(group + k, nj // 2) for k in range(1, nj // 2)]
    for p in peers:
        pl.semaphore_signal(barrier, inc=1, device_id=(p // 2, group * 2 + lax.rem(p, 2)),
                            device_id_type=MESH)
    for g in far_groups:
        for s in range(nr):
            pl.semaphore_signal(barrier, inc=1, device_id=(s, g * 2 + plane),
                                device_id_type=MESH)
        pl.semaphore_signal(barrier, inc=1, device_id=(r, g * 2 + 1 - plane),
                            device_id_type=MESH)
    greeted = np - 1 + (nj // 2 - 1) * (nr + 1)

    load([("v", v_hbm, vall.at[r, pl.ds(0, mb)]), ("s", s_hbm, sv), ("ev", ev_hbm, evv),
          ("ec", ec_hbm, ecv), ("call", c_hbm, call.at[:, j])])

    def remote(src, dst, send_sem, recv_sem, row, col):
        return pltpu.make_async_remote_copy(
            src_ref=src, dst_ref=dst, send_sem=send_sem, recv_sem=recv_sem,
            device_id=(row, col), device_id_type=MESH)

    def arrived(ref, sem):
        remote(ref, ref, col_send.at[0], sem, mate, j).wait_recv()

    def sent(ref, sem):
        remote(ref, ref, sem, col_recv.at[0], mate, j).wait_send()

    def val_block(s):
        return vall.at[s, pl.ds(0, mb)]

    def val_copy(s):
        return remote(v_hbm, val_block(r), val_send.at[s // 2], val_recv.at[r // 2], s, j)

    def pass_copy(s):
        return remote(val_block(s), val_block(s), pass_send.at[0], pass_recv.at[0], mate, j)

    def peer_copy(phase, src, dst, peer):
        return remote(src, dst, peer_send.at[phase], peer_recv.at[phase],
                      peer // 2, group * 2 + lax.rem(peer, 2))

    def owner_copy(phase, src, dst, q, g):
        return remote(src, dst, own_send.at[phase], own_recv.at[phase],
                      q * (nj // 2) + group, g * 2 + plane)

    groups = [lax.rem(group + k, nj // 2) for k in range(nj // 2)]

    def owner_each(q, g, away, here):
        if g is groups[0]:
            itself = q * (nj // 2) + group == r
            pl.when(jnp.logical_not(itself))(away)
            if here is not None:
                pl.when(itself)(here)
        else:
            away()

    def owner_send(phase, buffer, target, chosen):
        for g in chosen:
            for q in range(nq):
                def away():
                    owner_copy(phase, buffer.at[q], target.at[r], q, g).start()

                def here():
                    target[r] = buffer[q]

                owner_each(q, g, away, here)

    holder = lax.rem(r, nj // 2) * 2 + plane
    holds = holder == j

    def far_copy(g):
        return remote(w0, w0, far_send.at[0], far_recv.at[0], r, g * 2 + plane)

    def all_send(phase, src_of, dst):
        for p in peers:
            peer_copy(phase, src_of(p), dst, p).start()

    loads["c"].wait()
    loads["x"].wait()
    first = dot_nt(cv[...].reshape(nb, cw), xv[0].astype(BF16))
    asend[...] = first.astype(BF16).reshape(asend.shape)

    pl.semaphore_wait(barrier, greeted)
    owner_send(0, asend, arecv, groups[:1])
    for s in chips:
        val_copy(s).start()
    loads["v"].wait()
    pass_copy(r).start()

    loads["s"].wait()
    scr = sv[...].astype(F32)
    scr = jnp.concatenate([scr, jnp.zeros((LANES - mb, nb), F32)], axis=0)
    wide = -(-nb // LANES) * LANES
    if wide > nb:
        scr = jnp.concatenate([scr, jnp.zeros((LANES, wide - nb), F32)], axis=1)
    scr = scr.T
    st[...] = scr[:nb].astype(BF16).reshape(st.shape)
    owner_send(1, st, sall, groups[1:] + groups[:1])
    for s in col_peers:
        remote(c_hbm, call.at[:, j], col_send.at[0], col_recv.at[0], r, s).start()

    if mb < LANES:
        for i in range(nr):
            vall[i, pl.ds(mb, LANES - mb)] = jnp.zeros((LANES - mb, nv), BF16)
    for name in ("ev", "ec", "call"):
        loads[name].wait()
    evb[...] = jnp.broadcast_to(evv[...], (LANES, nv)).T
    ec = ecv[:, pl.ds(pl.multiple_of(r * cw, cw), cw)]

    def screen(w):
        allv = vall[...].reshape(nr * LANES, nv)
        inner = dot_nt(w, allv)
        tile = jnp.concatenate(
            [(sall[i].astype(F32) * inner[:, i * LANES:(i + 1) * LANES]).astype(BF16)
             for i in range(nr)], axis=1)
        return jnp.dot(tile, allv, preferred_element_type=F32).astype(BF16)

    mine = pl.ds(pl.multiple_of(plane * vh, vh), vh)
    b1t[...] = ((ec - evb[mine, :]) * xv[0, mine, :]).T

    @pl.when(holds)
    def _():
        arrived(arecv.at[pl.ds(0, nr - 1)], own_recv.at[0])
        total = arecv[0].astype(F32)
        for i in range(1, nr):
            total = total + arecv[i].astype(F32)
        w0[...] = total.astype(BF16)
        for g in groups[1:]:
            far_copy(g).start()

    for s in reversed(chips):
        arrived(val_block(s), val_recv.at[s // 2])
        pass_copy(s).start()

    @pl.when(holds)
    def _():
        arrived(sall.at[pl.ds(0, nr - 1)], own_recv.at[1])

    @pl.when(jnp.logical_not(holds))
    def _():
        arrived(sall, own_recv.at[1])
        arrived(w0, far_recv.at[0])

    arrived(vall.at[pl.ds(0, nr // 2), pl.ds(0, mb)], pass_recv.at[0])
    y0 = screen(w0[...])
    ysend0[0] = y0[:, :vh]
    ysend0[1] = y0[:, vh:]
    all_send(0, lambda p: ysend0.at[lax.rem(p, 2)], yall0.at[me])
    yall0[me] = ysend0[plane]
    arrived(call.at[:, pl.ds(0, nj - 1)], col_recv.at[0])
    condt[...] = call[...].reshape(np * nk, cw).T
    for s in chips:
        val_copy(s).wait_send()
    sent(vall.at[pl.ds(0, nr // 2), pl.ds(0, mb)], pass_send.at[0])
    sent(call.at[:, pl.ds(0, nj - 1)], col_send.at[0])

    @pl.when(holds)
    def _():
        sent(asend.at[pl.ds(0, nq - 1)], own_send.at[0])
        sent(sall.at[pl.ds(0, nr - 1)], own_send.at[1])
        sent(arecv.at[pl.ds(0, nj // 2 - 1)], far_send.at[0])

    @pl.when(jnp.logical_not(holds))
    def _():
        sent(asend, own_send.at[0])
        sent(sall, own_send.at[1])

    arrived(yall0.at[pl.ds(0, np - 1)], peer_recv.at[0])
    k0t = jnp.dot(condt[...], yall0[...].reshape(np * nk, vh), preferred_element_type=F32)
    x1t = (b1t[...] + k0t).astype(BF16)

    def kernel_block(p):
        cond = call[p // nj, lax.rem(p, nj)]
        esend[p] = jnp.dot(cond, x1t, preferred_element_type=F32).astype(BF16)

    for p in peers:
        kernel_block(p)
        peer_copy(1, esend.at[p], erecv.at[plane * nr + r], p).start()
    kernel_block(me)
    erecv[plane * nr + r] = esend[me]
    kz0[plane] = k0t.astype(BF16)

    other = group * 2 + 1 - plane
    swap = remote(kz0.at[plane], kz0.at[plane], mate_send.at[0], mate_recv.at[0], r, other)
    swap.start()
    sent(yall0.at[pl.ds(0, np - 1)], peer_send.at[0])
    arrived(erecv.at[pl.ds(0, np - 1)], peer_recv.at[1])

    halves = []
    for h in range(2):
        total = erecv[h * nr].astype(F32)
        for i in range(1, nr):
            total = total + erecv[h * nr + i].astype(F32)
        halves.append(total)
    ysend1[...] = screen(jnp.concatenate(halves, axis=1).astype(BF16))
    all_send(2, lambda p: ysend1, yall1.at[me])
    yall1[me] = ysend1[...]
    arrived(kz0.at[1 - plane], mate_recv.at[0])
    energy = ec - evb[...]
    k0 = jnp.concatenate([kz0[h].astype(F32).T for h in range(2)], axis=0)
    basev[0] = energy * (energy * xv[0] + k0)
    store = pltpu.make_async_copy(basev, base_hbm, local_sem.at[len(loads)])
    store.start()
    swap.wait_send()
    sent(erecv.at[pl.ds(0, np - 1)], peer_send.at[1])
    arrived(yall1.at[pl.ds(0, np - 1)], peer_recv.at[2])
    k1t = jnp.dot(condt[...], yall1[...].reshape(np * nk, nv), preferred_element_type=F32)
    k1_ref[0] = k1t.T
    store.wait()
    sent(yall1.at[pl.ds(0, np - 1)], peer_send.at[2])


def fused(nr, nj, trial, screened, val_points, cond_points, eps_val, eps_cond):
    mb, nv = val_points.shape
    nb, cw = cond_points.shape
    np = 2 * nr
    nq = np // nj
    nk = nb // nq
    vh = nv // 2
    ng = nj // 2
    scratch = [
        pltpu.VMEM(trial.shape, F32),
        pltpu.VMEM(screened.shape, BF16),
        pltpu.VMEM((nq, nk, cw), BF16),
        pltpu.VMEM((1, nv), F32),
        pltpu.VMEM((1, eps_cond.shape[0]), F32),
        pltpu.VMEM((nr, LANES, nv), BF16),
        pltpu.VMEM((nq, nk, LANES), BF16),
        pltpu.VMEM((nr, nk, LANES), BF16),
        pltpu.VMEM((nq, nk, nv), BF16),
        pltpu.VMEM((nr, nk, nv), BF16),
        pltpu.VMEM((nq, nj, nk, cw), BF16),
        pltpu.VMEM((nv, LANES), F32),
        pltpu.VMEM((2, nk, vh), BF16),
        pltpu.VMEM((nk, nv), BF16),
        pltpu.VMEM((np, nk, vh), BF16),
        pltpu.VMEM((np, nk, nv), BF16),
        pltpu.VMEM((np, nk, vh), BF16),
        pltpu.VMEM((np, nk, vh), BF16),
        pltpu.VMEM((2, cw, vh), BF16),
        pltpu.VMEM((nk, nv), BF16),
        pltpu.VMEM((cw, vh), F32),
        pltpu.VMEM((cw, np * nk), BF16),
        pltpu.VMEM(trial.shape, F32),
        pltpu.SemaphoreType.DMA((8,)),
        pltpu.SemaphoreType.DMA((2,)),
        pltpu.SemaphoreType.DMA((2,)),
        pltpu.SemaphoreType.DMA((1,)),
        pltpu.SemaphoreType.DMA((1,)),
        pltpu.SemaphoreType.DMA((3,)),
        pltpu.SemaphoreType.DMA((3,)),
        pltpu.SemaphoreType.DMA((1,)),
        pltpu.SemaphoreType.DMA((1,)),
        pltpu.SemaphoreType.DMA((1,)),
        pltpu.SemaphoreType.DMA((1,)),
        pltpu.SemaphoreType.DMA((nr // 2,)),
        pltpu.SemaphoreType.DMA((nr // 2,)),
        pltpu.SemaphoreType.DMA((1,)),
        pltpu.SemaphoreType.DMA((1,)),
    ]
    base, last = pl.pallas_call(
        functools.partial(kernel, nr, nj),
        out_shape=(jax.ShapeDtypeStruct(trial.shape, F32),) * 2,
        in_specs=[pl.BlockSpec(memory_space=pltpu.HBM)] * 6,
        out_specs=(pl.BlockSpec(memory_space=pltpu.HBM), pl.BlockSpec(memory_space=pltpu.VMEM)),
        scratch_shapes=scratch,
        compiler_params=pltpu.CompilerParams(
            collective_id=0, has_side_effects=True, vmem_limit_bytes=64 * 2**20 - 65536),
    )(trial, screened, val_points, cond_points.reshape(nq, nk, cw), eps_val[None], eps_cond[None])
    return base + last


def fits(nr, nj, trial, val_points, cond_points):
    mb, nv = val_points.shape
    nb, cw = cond_points.shape
    if nr % 2 or nj % 2 or (2 * nr) % nj or nb % (2 * nr // nj):
        return False
    nk = nb // (2 * nr // nj)
    return (trial.shape[0] == 1 and cw == LANES and nk % ROWS16 == 0
            and mb % ROWS16 == 0 and mb <= LANES and nv == 2 * LANES)


def general(trial, screened, val_points, cond_points, eps_val, eps_cond):
    cond_full = lax.all_gather(cond_points, "row", axis=1, tiled=True)
    energy_full = eps_cond[None, :] - eps_val[:, None]
    width = trial.shape[2]
    offset = lax.axis_index("row") * width
    x_full = lax.all_gather(trial.astype(BF16), "row", axis=2, tiled=True).astype(trial.dtype)
    xb_full = x_full.astype(BF16)
    x_mine = trial
    for step in range(APPLY):
        pair = jnp.einsum(
            "mv,bvc->bmc", val_points, xb_full, preferred_element_type=F32).astype(BF16)
        inner = jnp.einsum("bmc,nc->bmn", pair, cond_full, preferred_element_type=F32)
        tile = (screened[None] * inner).astype(BF16)
        back = jnp.einsum("bmn,nc->bmc", tile, cond_full, preferred_element_type=F32).astype(BF16)
        part_low = jnp.einsum(
            "mv,bmc->bvc", val_points, back, preferred_element_type=F32).astype(BF16)
        partial_terms = lax.optimization_barrier(part_low).astype(F32)
        kernel_full = lax.psum(partial_terms, ("row", "col"))
        x_full = energy_full[None] * x_full + kernel_full
        xb_full = x_full.astype(BF16)
        x_mine = lax.dynamic_slice_in_dim(x_full, offset, width, 2)
    return x_mine


def solution(mesh):
    nr, nj = mesh.shape["row"], mesh.shape["col"]

    def body(trial, screened, val_points, cond_points, eps_val, eps_cond):
        args = (trial, screened, val_points, cond_points, eps_val, eps_cond)
        if fits(nr, nj, trial, val_points, cond_points):
            return fused(nr, nj, *args)
        return general(*args)

    in_specs = (P(None, None, "row"), P("row", "col"), P("row", None), P("col", "row"), P(), P())
    out_specs = P(None, None, "row")
    return jax.shard_map(body, mesh=mesh, in_specs=in_specs, out_specs=out_specs, check_vma=False)
```

time: 36.3 us -> 34.2 us (0.942)
  Pallas kernels: 34.6 us -> 32.4 us
  other arithmetic: 0 us -> 1.64 us
  local copies, waits for them, and re-layouts: 1.57 us -> 0 us
    pallas_call x1, Pallas kernels: 34.6 us -> 32.4 us  [fused(): pl.pallas_call(functools.partial(kernel, nr, nj), out_shape=(jax.ShapeDty...]
    add x0 -> x1, other arithmetic: none -> 1.64 us  [fused(): return base + last]
    unnamed x1 -> x0, local copies, waits for them, and re-layouts: 1.57 us -> none
where the time goes in v4:
time: 34.2 us; the launch traced here: 34 us
  Pallas kernels  32.4 us (95%)
  other arithmetic  1.64 us (5%)
    pallas_call x1, Pallas kernels, fused(): pl.pallas_call(functools.partial(kernel, nr, nj), out_shape=(jax.ShapeDty...  32.4 us
    add x1, other arithmetic, fused(): return base + last  1.64 us

profile of v4, /device:TPU:0, one launch (start us, length us, event | category | flops | bytes accessed | tf_op | source)
XLA Modules:
  0.0 34.0 jit_solution(6619684340135968650)
XLA Ops:
  0.0 32.4 %shard_map.64 = (f32[1,256,128]{2,1,0:T(8,128)}, f32[1,256,128]{2,1,0:T(8,128)}) custom-call(f32[1,256,128]{2,1,0:T(8,128)} %x_hbm.1, bf16[96,192]{1,0:T(8,128)(2,1)} %s_hbm.1, bf16[96,256]{1,0:T(8,128)(2,1)} %v_hbm.1, bf16[4,48,128]{2,1,0:T(8,128)(2,1)} %bitcast.3, f32[1,256]{1,0:T(1,128)} %bitcast.5, f32[1,1024]{1,0:T(1,128)} %bitcast.4), custom_call_target="tpu_custom_call" | custom-call | tf_op jit(solution)/shard_map/pallas_call | solution.py:311
  32.4 1.6 %add.3 = f32[1,256,128]{2,1,0:T(8,128)} add(f32[1,256,128]{2,1,0:T(8,128)} %get-tuple-element.7, f32[1,256,128]{2,1,0:T(8,128)} %get-tuple-element.8) | non-fusion elementwise | flops 32768 | bytes 393216 | tf_op jit(solution)/shard_map/add | solution.py:320

commit v5 on v4

--- a/solution.py
+++ b/solution.py
@@ -19,9 +19,9 @@
     return lax.dot_general(a, b, (((1,), (1,)), ((), ())), preferred_element_type=F32)
 
 
-def kernel(nr, nj, x_hbm, s_hbm, v_hbm, c_hbm, ev_hbm, ec_hbm, base_hbm, k1_ref,
+def kernel(nr, nj, x_hbm, s_hbm, v_hbm, c_hbm, ev_hbm, ec_hbm, out_ref,
            xv, sv, cv, evv, ecv, vall, st, sall, asend, arecv, call, evb,
-           ysend0, ysend1, yall0, yall1, esend, erecv, kz0, w0, b1t, condt, basev,
+           ysend0, ysend1, yall0, yall1, esend, erecv, kz0, w0, b1t, condt,
            local_sem, own_send, own_recv, col_send, col_recv, peer_send, peer_recv,
            mate_send, mate_recv, far_send, far_recv,
            val_send, val_recv, pass_send, pass_recv):
@@ -248,15 +248,12 @@
     arrived(kz0.at[1 - plane], mate_recv.at[0])
     energy = ec - evb[...]
     k0 = jnp.concatenate([kz0[h].astype(F32).T for h in range(2)], axis=0)
-    basev[0] = energy * (energy * xv[0] + k0)
-    store = pltpu.make_async_copy(basev, base_hbm, local_sem.at[len(loads)])
-    store.start()
+    out_ref[0] = energy * (energy * xv[0] + k0)
     swap.wait_send()
     sent(erecv.at[pl.ds(0, np - 1)], peer_send.at[1])
     arrived(yall1.at[pl.ds(0, np - 1)], peer_recv.at[2])
     k1t = jnp.dot(condt[...], yall1[...].reshape(np * nk, nv), preferred_element_type=F32)
-    k1_ref[0] = k1t.T
-    store.wait()
+    out_ref[0] += k1t.T
     sent(yall1.at[pl.ds(0, np - 1)], peer_send.at[2])
 
 
@@ -291,8 +288,7 @@
         pltpu.VMEM((nk, nv), BF16),
         pltpu.VMEM((cw, vh), F32),
         pltpu.VMEM((cw, np * nk), BF16),
-        pltpu.VMEM(trial.shape, F32),
-        pltpu.SemaphoreType.DMA((8,)),
+        pltpu.SemaphoreType.DMA((7,)),
         pltpu.SemaphoreType.DMA((2,)),
         pltpu.SemaphoreType.DMA((2,)),
         pltpu.SemaphoreType.DMA((1,)),
@@ -308,16 +304,15 @@
         pltpu.SemaphoreType.DMA((1,)),
         pltpu.SemaphoreType.DMA((1,)),
     ]
-    base, last = pl.pallas_call(
+    return pl.pallas_call(
         functools.partial(kernel, nr, nj),
-        out_shape=(jax.ShapeDtypeStruct(trial.shape, F32),) * 2,
+        out_shape=pltpu.VMEM(trial.shape, F32),
         in_specs=[pl.BlockSpec(memory_space=pltpu.HBM)] * 6,
-        out_specs=(pl.BlockSpec(memory_space=pltpu.HBM), pl.BlockSpec(memory_space=pltpu.VMEM)),
+        out_specs=pl.BlockSpec(memory_space=pltpu.VMEM),
         scratch_shapes=scratch,
         compiler_params=pltpu.CompilerParams(
-            collective_id=0, has_side_effects=True, vmem_limit_bytes=64 * 2**20 - 65536),
+            collective_id=0, has_side_effects=True, vmem_limit_bytes=64 * 2**20 - 2**18),
     )(trial, screened, val_points, cond_points.reshape(nq, nk, cw), eps_val[None], eps_cond[None])
-    return base + last
 
 
 def fits(nr, nj, trial, val_points, cond_points):

time: 34.2 us -> 32.5 us (0.950)
  other arithmetic: 1.64 us -> 0 us
  Pallas kernels: 32.4 us -> 31.7 us
  local copies, waits for them, and re-layouts: 0 us -> 0.66 us
    add x1 -> x0, other arithmetic: 1.64 us -> none  [fused(): return base + last]
    pallas_call x1, Pallas kernels: 32.4 us -> 31.7 us  [fused(): pl.pallas_call(functools.partial(kernel, nr, nj), out_shape=pltpu.VMEM(tr...]
    unnamed x0 -> x1, local copies, waits for them, and re-layouts: none -> 0.66 us
where the time goes in v5:
time: 32.5 us; the launch traced here: 32.4 us
  Pallas kernels  31.7 us (98%)
  local copies, waits for them, and re-layouts  0.66 us (2%)
    pallas_call x1, Pallas kernels, fused(): pl.pallas_call(functools.partial(kernel, nr, nj), out_shape=pltpu.VMEM(tr...  31.7 us
    unnamed x1, local copies, waits for them, and re-layouts  0.66 us

profile of v5, /device:TPU:0, one launch (start us, length us, event | category | flops | bytes accessed | tf_op | source)
XLA Modules:
  0.0 32.4 jit_solution(8909337292278302053)
XLA Ops:
  0.0 31.7 %shard_map.64 = f32[1,256,128]{2,1,0:T(8,128)S(1)} custom-call(f32[1,256,128]{2,1,0:T(8,128)} %x_hbm.1, bf16[96,192]{1,0:T(8,128)(2,1)} %s_hbm.1, bf16[96,256]{1,0:T(8,128)(2,1)} %v_hbm.1, bf16[4,48,128]{2,1,0:T(8,128)(2,1)} %bitcast.3, f32[1,256]{1,0:T(1,128)} %bitcast.5, f32[1,1024]{1,0:T(1,128)} %bitcast.4), custom_call_target="tpu_custom_call" | custom-call | tf_op jit(solution)/shard_map/pallas_call | solution.py:307
  31.7 0.7 %copy.8 = f32[1,256,128]{2,1,0:T(8,128)} copy(f32[1,256,128]{2,1,0:T(8,128)S(1)} %shard_map.64) | data formatting | bytes 262144

commit v6 on v5

--- a/solution.py
+++ b/solution.py
@@ -219,14 +219,9 @@
     k0t = jnp.dot(condt[...], yall0[...].reshape(np * nk, vh), preferred_element_type=F32)
     x1t = (b1t[...] + k0t).astype(BF16)
 
-    def kernel_block(p):
-        cond = call[p // nj, lax.rem(p, nj)]
-        esend[p] = jnp.dot(cond, x1t, preferred_element_type=F32).astype(BF16)
-
-    for p in peers:
-        kernel_block(p)
-        peer_copy(1, esend.at[p], erecv.at[plane * nr + r], p).start()
-    kernel_block(me)
+    cond = call[...].reshape(np * nk, cw)
+    esend[...] = jnp.dot(cond, x1t, preferred_element_type=F32).astype(BF16).reshape(esend.shape)
+    all_send(1, lambda p: esend.at[p], erecv.at[plane * nr + r])
     erecv[plane * nr + r] = esend[me]
     kz0[plane] = k0t.astype(BF16)
 

time: 32.5 us -> 31.9 us (0.982)
  Pallas kernels: 31.7 us -> 31.1 us
    pallas_call x1, Pallas kernels: 31.7 us -> 31.1 us  [fused(): pl.pallas_call(functools.partial(kernel, nr, nj), out_shape=pltpu.VMEM(tr...]
where the time goes in v6:
time: 31.9 us; the launch traced here: 31.7 us
  Pallas kernels  31.1 us (97%)
  local copies, waits for them, and re-layouts  0.66 us (2%)
    pallas_call x1, Pallas kernels, fused(): pl.pallas_call(functools.partial(kernel, nr, nj), out_shape=pltpu.VMEM(tr...  31.1 us
    unnamed x1, local copies, waits for them, and re-layouts  0.66 us

profile of v6, /device:TPU:0, one launch (start us, length us, event | category | flops | bytes accessed | tf_op | source)
XLA Modules:
  0.0 31.7 jit_solution(11814100389963212948)
XLA Ops:
  0.0 31.1 %shard_map.64 = f32[1,256,128]{2,1,0:T(8,128)S(1)} custom-call(f32[1,256,128]{2,1,0:T(8,128)} %x_hbm.1, bf16[96,192]{1,0:T(8,128)(2,1)} %s_hbm.1, bf16[96,256]{1,0:T(8,128)(2,1)} %v_hbm.1, bf16[4,48,128]{2,1,0:T(8,128)(2,1)} %bitcast.3, f32[1,256]{1,0:T(1,128)} %bitcast.5, f32[1,1024]{1,0:T(1,128)} %bitcast.4), custom_call_target="tpu_custom_call" | custom-call | tf_op jit(solution)/shard_map/pallas_call | solution.py:302
  31.1 0.7 %copy.8 = f32[1,256,128]{2,1,0:T(8,128)} copy(f32[1,256,128]{2,1,0:T(8,128)S(1)} %shard_map.64) | data formatting | bytes 262144

commit v7 on v6

--- a/solution.py
+++ b/solution.py
@@ -24,7 +24,8 @@
            ysend0, ysend1, yall0, yall1, esend, erecv, kz0, w0, b1t, condt,
            local_sem, own_send, own_recv, col_send, col_recv, peer_send, peer_recv,
            mate_send, mate_recv, far_send, far_recv,
-           val_send, val_recv, pass_send, pass_recv):
+           val_send, val_recv, pass_send, pass_recv,
+           last_send, last_recv, hand_send, hand_recv):
     r = lax.axis_index("row")
     j = lax.axis_index("col")
     group, plane = j // 2, lax.rem(j, 2)
@@ -238,7 +239,17 @@
             total = total + erecv[h * nr + i].astype(F32)
         halves.append(total)
     ysend1[...] = screen(jnp.concatenate(halves, axis=1).astype(BF16))
-    all_send(2, lambda p: ysend1, yall1.at[me])
+    def cross(s, p):
+        return remote(ysend1, yall1.at[me], last_send.at[0],
+                      last_recv.at[r // 2 * 2 + plane], s, group * 2 + p)
+
+    def hand(src, p):
+        return remote(src, yall1.at[p], hand_send.at[0], hand_recv.at[0], mate, j)
+
+    others = ([(s, p) for s in chips for p in (1 - plane, plane)] + [(r, 1 - plane)])
+    for s, p in others:
+        cross(s, p).start()
+    hand(ysend1, me).start()
     yall1[me] = ysend1[...]
     arrived(kz0.at[1 - plane], mate_recv.at[0])
     energy = ec - evb[...]
@@ -246,10 +257,17 @@
     out_ref[0] = energy * (energy * xv[0] + k0)
     swap.wait_send()
     sent(erecv.at[pl.ds(0, np - 1)], peer_send.at[1])
-    arrived(yall1.at[pl.ds(0, np - 1)], peer_recv.at[2])
+    sources = ([(lax.rem(r + nr - 2 * k, nr), p) for k in range(1, nr // 2)
+                for p in (1 - plane, plane)])
+    for s, p in [(r, 1 - plane)] + sources:
+        block = yall1.at[s * 2 + p]
+        arrived(block, last_recv.at[s // 2 * 2 + p])
+        hand(block, s * 2 + p).start()
+    arrived(yall1.at[pl.ds(0, nr)], hand_recv.at[0])
     k1t = jnp.dot(condt[...], yall1[...].reshape(np * nk, nv), preferred_element_type=F32)
     out_ref[0] += k1t.T
-    sent(yall1.at[pl.ds(0, np - 1)], peer_send.at[2])
+    sent(yall1.at[pl.ds(0, nr - 1)], last_send.at[0])
+    sent(yall1.at[pl.ds(0, nr)], hand_send.at[0])
 
 
 def fused(nr, nj, trial, screened, val_points, cond_points, eps_val, eps_cond):
@@ -288,14 +306,18 @@
         pltpu.SemaphoreType.DMA((2,)),
         pltpu.SemaphoreType.DMA((1,)),
         pltpu.SemaphoreType.DMA((1,)),
-        pltpu.SemaphoreType.DMA((3,)),
-        pltpu.SemaphoreType.DMA((3,)),
+        pltpu.SemaphoreType.DMA((2,)),
+        pltpu.SemaphoreType.DMA((2,)),
         pltpu.SemaphoreType.DMA((1,)),
         pltpu.SemaphoreType.DMA((1,)),
         pltpu.SemaphoreType.DMA((1,)),
         pltpu.SemaphoreType.DMA((1,)),
         pltpu.SemaphoreType.DMA((nr // 2,)),
         pltpu.SemaphoreType.DMA((nr // 2,)),
+        pltpu.SemaphoreType.DMA((1,)),
+        pltpu.SemaphoreType.DMA((1,)),
+        pltpu.SemaphoreType.DMA((1,)),
+        pltpu.SemaphoreType.DMA((nr,)),
         pltpu.SemaphoreType.DMA((1,)),
         pltpu.SemaphoreType.DMA((1,)),
     ]

time: 31.9 us -> 30.8 us (0.966)
  Pallas kernels: 31.1 us -> 29.8 us
    pallas_call x1, Pallas kernels: 31.1 us -> 29.8 us  [fused(): pl.pallas_call(functools.partial(kernel, nr, nj), out_shape=pltpu.VMEM(tr...]
where the time goes in v7:
time: 30.8 us; the launch traced here: 30.4 us
  Pallas kernels  29.8 us (97%)
  local copies, waits for them, and re-layouts  0.66 us (2%)
    pallas_call x1, Pallas kernels, fused(): pl.pallas_call(functools.partial(kernel, nr, nj), out_shape=pltpu.VMEM(tr...  29.8 us
    unnamed x1, local copies, waits for them, and re-layouts  0.66 us

profile of v7, /device:TPU:0, one launch (start us, length us, event | category | flops | bytes accessed | tf_op | source)
XLA Modules:
  0.0 30.4 jit_solution(4078446553514261287)
XLA Ops:
  0.0 29.8 %shard_map.64 = f32[1,256,128]{2,1,0:T(8,128)S(1)} custom-call(f32[1,256,128]{2,1,0:T(8,128)} %x_hbm.1, bf16[96,192]{1,0:T(8,128)(2,1)} %s_hbm.1, bf16[96,256]{1,0:T(8,128)(2,1)} %v_hbm.1, bf16[4,48,128]{2,1,0:T(8,128)(2,1)} %bitcast.3, f32[1,256]{1,0:T(1,128)} %bitcast.5, f32[1,1024]{1,0:T(1,128)} %bitcast.4), custom_call_target="tpu_custom_call" | custom-call | tf_op jit(solution)/shard_map/pallas_call | solution.py:324
  29.8 0.7 %copy.8 = f32[1,256,128]{2,1,0:T(8,128)} copy(f32[1,256,128]{2,1,0:T(8,128)S(1)} %shard_map.64) | data formatting | bytes 262144

commit v8 on v7

--- a/solution.py
+++ b/solution.py
@@ -32,6 +32,16 @@
     me = r * 2 + plane
     np = nr * 2
     nq = np // nj
+    nh = nr // 2
+    core = lax.rem(r, 2)
+
+    def row_at(s):
+        return lax.rem(s, 2) * nh + s // 2
+
+    def peer_at(p):
+        return lax.rem(p // 2, 2) * nr + p // 4 * 2 + lax.rem(p, 2)
+
+    here_at = peer_at(me)
     mb, nv = v_hbm.shape
     _, nk, cw = c_hbm.shape
     nb = nq * nk
@@ -52,19 +62,19 @@
     mate = r + 1 - 2 * lax.rem(r, 2)
     col_peers = [lax.rem(j + k, nj) for k in range(1, nj)]
     far_groups = [lax.rem(group + k, nj // 2) for k in range(1, nj // 2)]
-    for p in peers:
-        pl.semaphore_signal(barrier, inc=1, device_id=(p // 2, group * 2 + lax.rem(p, 2)),
-                            device_id_type=MESH)
     for g in far_groups:
         for s in range(nr):
             pl.semaphore_signal(barrier, inc=1, device_id=(s, g * 2 + plane),
                                 device_id_type=MESH)
         pl.semaphore_signal(barrier, inc=1, device_id=(r, g * 2 + 1 - plane),
                             device_id_type=MESH)
+    for p in peers:
+        pl.semaphore_signal(barrier, inc=1, device_id=(p // 2, group * 2 + lax.rem(p, 2)),
+                            device_id_type=MESH)
     greeted = np - 1 + (nj // 2 - 1) * (nr + 1)
 
-    load([("v", v_hbm, vall.at[r, pl.ds(0, mb)]), ("s", s_hbm, sv), ("ev", ev_hbm, evv),
-          ("ec", ec_hbm, ecv), ("call", c_hbm, call.at[:, j])])
+    load([("v", v_hbm, vall.at[row_at(r), pl.ds(0, mb)]), ("s", s_hbm, sv), ("ev", ev_hbm, evv),
+          ("ec", ec_hbm, ecv), ("call", c_hbm, call.at[j // 2, :, lax.rem(j, 2)])])
 
     def remote(src, dst, send_sem, recv_sem, row, col):
         return pltpu.make_async_remote_copy(
@@ -78,7 +88,7 @@
         remote(ref, ref, sem, col_recv.at[0], mate, j).wait_send()
 
     def val_block(s):
-        return vall.at[s, pl.ds(0, mb)]
+        return vall.at[row_at(s), pl.ds(0, mb)]
 
     def val_copy(s):
         return remote(v_hbm, val_block(r), val_send.at[s // 2], val_recv.at[r // 2], s, j)
@@ -105,14 +115,14 @@
         else:
             away()
 
-    def owner_send(phase, buffer, target, chosen):
+    def owner_send(phase, buffer, target, slot, chosen):
         for g in chosen:
             for q in range(nq):
                 def away():
-                    owner_copy(phase, buffer.at[q], target.at[r], q, g).start()
+                    owner_copy(phase, buffer.at[q], target.at[slot], q, g).start()
 
                 def here():
-                    target[r] = buffer[q]
+                    target[slot] = buffer[q]
 
                 owner_each(q, g, away, here)
 
@@ -132,7 +142,7 @@
     asend[...] = first.astype(BF16).reshape(asend.shape)
 
     pl.semaphore_wait(barrier, greeted)
-    owner_send(0, asend, arecv, groups[:1])
+    owner_send(0, asend, arecv, r, groups[:1])
     for s in chips:
         val_copy(s).start()
     loads["v"].wait()
@@ -146,9 +156,9 @@
         scr = jnp.concatenate([scr, jnp.zeros((LANES, wide - nb), F32)], axis=1)
     scr = scr.T
     st[...] = scr[:nb].astype(BF16).reshape(st.shape)
-    owner_send(1, st, sall, groups[1:] + groups[:1])
+    owner_send(1, st, sall, row_at(r), groups[1:] + groups[:1])
     for s in col_peers:
-        remote(c_hbm, call.at[:, j], col_send.at[0], col_recv.at[0], r, s).start()
+        remote(c_hbm, call.at[j // 2, :, lax.rem(j, 2)], col_send.at[0], col_recv.at[0], r, s).start()
 
     if mb < LANES:
         for i in range(nr):
@@ -158,13 +168,13 @@
     evb[...] = jnp.broadcast_to(evv[...], (LANES, nv)).T
     ec = ecv[:, pl.ds(pl.multiple_of(r * cw, cw), cw)]
 
-    def screen(w):
-        allv = vall[...].reshape(nr * LANES, nv)
+    def screen_half(w, h):
+        allv = vall[pl.ds(h * nh, nh)].reshape(nh * LANES, nv)
         inner = dot_nt(w, allv)
         tile = jnp.concatenate(
-            [(sall[i].astype(F32) * inner[:, i * LANES:(i + 1) * LANES]).astype(BF16)
-             for i in range(nr)], axis=1)
-        return jnp.dot(tile, allv, preferred_element_type=F32).astype(BF16)
+            [(sall[h * nh + i].astype(F32) * inner[:, i * LANES:(i + 1) * LANES]).astype(BF16)
+             for i in range(nh)], axis=1)
+        return jnp.dot(tile, allv, preferred_element_type=F32)
 
     mine = pl.ds(pl.multiple_of(plane * vh, vh), vh)
     b1t[...] = ((ec - evb[mine, :]) * xv[0, mine, :]).T
@@ -192,18 +202,20 @@
         arrived(sall, own_recv.at[1])
         arrived(w0, far_recv.at[0])
 
-    arrived(vall.at[pl.ds(0, nr // 2), pl.ds(0, mb)], pass_recv.at[0])
-    y0 = screen(w0[...])
+    w = w0[...]
+    y0 = screen_half(w, core)
+    arrived(vall.at[pl.ds(0, nh), pl.ds(0, mb)], pass_recv.at[0])
+    y0 = (y0 + screen_half(w, 1 - core)).astype(BF16)
     ysend0[0] = y0[:, :vh]
     ysend0[1] = y0[:, vh:]
-    all_send(0, lambda p: ysend0.at[lax.rem(p, 2)], yall0.at[me])
-    yall0[me] = ysend0[plane]
-    arrived(call.at[:, pl.ds(0, nj - 1)], col_recv.at[0])
+    all_send(0, lambda p: ysend0.at[lax.rem(p, 2)], yall0.at[here_at])
+    yall0[here_at] = ysend0[plane]
+    arrived(esend.at[pl.ds(0, nq * (nj - 1))], col_recv.at[0])
     condt[...] = call[...].reshape(np * nk, cw).T
     for s in chips:
         val_copy(s).wait_send()
     sent(vall.at[pl.ds(0, nr // 2), pl.ds(0, mb)], pass_send.at[0])
-    sent(call.at[:, pl.ds(0, nj - 1)], col_send.at[0])
+    sent(esend.at[pl.ds(0, nq * (nj - 1))], col_send.at[0])
 
     @pl.when(holds)
     def _():
@@ -222,8 +234,8 @@
 
     cond = call[...].reshape(np * nk, cw)
     esend[...] = jnp.dot(cond, x1t, preferred_element_type=F32).astype(BF16).reshape(esend.shape)
-    all_send(1, lambda p: esend.at[p], erecv.at[plane * nr + r])
-    erecv[plane * nr + r] = esend[me]
+    all_send(1, lambda p: esend.at[peer_at(p)], erecv.at[plane * nr + r])
+    erecv[plane * nr + r] = esend[here_at]
     kz0[plane] = k0t.astype(BF16)
 
     other = group * 2 + 1 - plane
@@ -238,19 +250,20 @@
         for i in range(1, nr):
             total = total + erecv[h * nr + i].astype(F32)
         halves.append(total)
-    ysend1[...] = screen(jnp.concatenate(halves, axis=1).astype(BF16))
+    w = jnp.concatenate(halves, axis=1).astype(BF16)
+    ysend1[...] = (screen_half(w, core) + screen_half(w, 1 - core)).astype(BF16)
     def cross(s, p):
-        return remote(ysend1, yall1.at[me], last_send.at[0],
+        return remote(ysend1, yall1.at[here_at], last_send.at[0],
                       last_recv.at[r // 2 * 2 + plane], s, group * 2 + p)
 
     def hand(src, p):
-        return remote(src, yall1.at[p], hand_send.at[0], hand_recv.at[0], mate, j)
+        return remote(src, yall1.at[peer_at(p)], hand_send.at[0], hand_recv.at[0], mate, j)
 
     others = ([(s, p) for s in chips for p in (1 - plane, plane)] + [(r, 1 - plane)])
     for s, p in others:
         cross(s, p).start()
     hand(ysend1, me).start()
-    yall1[me] = ysend1[...]
+    yall1[here_at] = ysend1[...]
     arrived(kz0.at[1 - plane], mate_recv.at[0])
     energy = ec - evb[...]
     k0 = jnp.concatenate([kz0[h].astype(F32).T for h in range(2)], axis=0)
@@ -260,12 +273,18 @@
     sources = ([(lax.rem(r + nr - 2 * k, nr), p) for k in range(1, nr // 2)
                 for p in (1 - plane, plane)])
     for s, p in [(r, 1 - plane)] + sources:
-        block = yall1.at[s * 2 + p]
+        block = yall1.at[peer_at(s * 2 + p)]
         arrived(block, last_recv.at[s // 2 * 2 + p])
         hand(block, s * 2 + p).start()
+
+    def last_half(h):
+        columns = pl.ds(pl.multiple_of(h * (nr * nk), LANES), nr * nk)
+        blocks = yall1[pl.ds(h * nr, nr)].reshape(nr * nk, nv)
+        return jnp.dot(condt[:, columns], blocks, preferred_element_type=F32).T
+
+    out_ref[0] += last_half(core)
     arrived(yall1.at[pl.ds(0, nr)], hand_recv.at[0])
-    k1t = jnp.dot(condt[...], yall1[...].reshape(np * nk, nv), preferred_element_type=F32)
-    out_ref[0] += k1t.T
+    out_ref[0] += last_half(1 - core)
     sent(yall1.at[pl.ds(0, nr - 1)], last_send.at[0])
     sent(yall1.at[pl.ds(0, nr)], hand_send.at[0])
 
@@ -289,7 +308,7 @@
         pltpu.VMEM((nr, nk, LANES), BF16),
         pltpu.VMEM((nq, nk, nv), BF16),
         pltpu.VMEM((nr, nk, nv), BF16),
-        pltpu.VMEM((nq, nj, nk, cw), BF16),
+        pltpu.VMEM((ng, nq, 2, nk, cw), BF16),
         pltpu.VMEM((nv, LANES), F32),
         pltpu.VMEM((2, nk, vh), BF16),
         pltpu.VMEM((nk, nv), BF16),
@@ -339,7 +358,8 @@
         return False
     nk = nb // (2 * nr // nj)
     return (trial.shape[0] == 1 and cw == LANES and nk % ROWS16 == 0
-            and mb % ROWS16 == 0 and mb <= LANES and nv == 2 * LANES)
+            and mb % ROWS16 == 0 and mb <= LANES and nv == 2 * LANES
+            and nj // 2 == 2 and nr * nk % LANES == 0)
 
 
 def general(trial, screened, val_points, cond_points, eps_val, eps_cond):

time: 30.8 us -> 31 us (level)
  no operation moved by 1% of the time
where the time goes in v8:
time: 31 us; the launch traced here: 30.7 us
  Pallas kernels  30 us (97%)
  local copies, waits for them, and re-layouts  0.66 us (2%)
    pallas_call x1, Pallas kernels, fused(): pl.pallas_call(functools.partial(kernel, nr, nj), out_shape=pltpu.VMEM(tr...  30 us
    unnamed x1, local copies, waits for them, and re-layouts  0.66 us

profile of v8, /device:TPU:0, one launch (start us, length us, event | category | flops | bytes accessed | tf_op | source)
XLA Modules:
  0.0 30.7 jit_solution(13971071146293005613)
XLA Ops:
  0.0 30.0 %shard_map.64 = f32[1,256,128]{2,1,0:T(8,128)S(1)} custom-call(f32[1,256,128]{2,1,0:T(8,128)} %x_hbm.1, bf16[96,192]{1,0:T(8,128)(2,1)} %s_hbm.1, bf16[96,256]{1,0:T(8,128)(2,1)} %v_hbm.1, bf16[4,48,128]{2,1,0:T(8,128)(2,1)} %bitcast.3, f32[1,256]{1,0:T(1,128)} %bitcast.5, f32[1,1024]{1,0:T(1,128)} %bitcast.4), custom_call_target="tpu_custom_call" | custom-call | tf_op jit(solution)/shard_map/pallas_call | solution.py:343
  30.1 0.7 %copy.8 = f32[1,256,128]{2,1,0:T(8,128)} copy(f32[1,256,128]{2,1,0:T(8,128)S(1)} %shard_map.64) | data formatting | bytes 262144

commit v9 on v7

--- a/solution.py
+++ b/solution.py
@@ -17,6 +17,10 @@
 
 def dot_nt(a, b):
     return lax.dot_general(a, b, (((1,), (1,)), ((), ())), preferred_element_type=F32)
+
+
+def wrap(x, n):
+    return lax.select(x >= n, x - n, x)
 
 
 def kernel(nr, nj, x_hbm, s_hbm, v_hbm, c_hbm, ev_hbm, ec_hbm, out_ref,
@@ -46,21 +50,23 @@
 
     load([("c", c_hbm, cv), ("x", x_hbm, xv)])
     barrier = pltpu.get_barrier_semaphore()
-    steps = sorted(range(1, np), key=lambda k: abs(k - np // 2))
-    peers = [lax.rem(me + k, np) for k in steps]
-    chips = [lax.rem(r + 2 * k, nr) for k in range(1, nr // 2)]
+    across = group * 2 + 1 - plane
+    planes = [(1 - plane, across), (plane, j)]
+    row_steps = sorted(range(nr), key=lambda k: abs(k - nr // 2))
+    rows = {k: wrap(r + k, nr) if k else r for k in range(nr)}
+    peers = [(rows[k], p, col) for k in row_steps for p, col in planes if k or col is across]
+    chips = [rows[2 * k] for k in range(1, nr // 2)]
     mate = r + 1 - 2 * lax.rem(r, 2)
-    col_peers = [lax.rem(j + k, nj) for k in range(1, nj)]
-    far_groups = [lax.rem(group + k, nj // 2) for k in range(1, nj // 2)]
-    for p in peers:
-        pl.semaphore_signal(barrier, inc=1, device_id=(p // 2, group * 2 + lax.rem(p, 2)),
-                            device_id_type=MESH)
+    col_peers = [wrap(j + k, nj) for k in range(1, nj)]
+    far_groups = [wrap(group + k, nj // 2) for k in range(1, nj // 2)]
     for g in far_groups:
         for s in range(nr):
             pl.semaphore_signal(barrier, inc=1, device_id=(s, g * 2 + plane),
                                 device_id_type=MESH)
         pl.semaphore_signal(barrier, inc=1, device_id=(r, g * 2 + 1 - plane),
                             device_id_type=MESH)
+    for s, p, col in peers:
+        pl.semaphore_signal(barrier, inc=1, device_id=(s, col), device_id_type=MESH)
     greeted = np - 1 + (nj // 2 - 1) * (nr + 1)
 
     load([("v", v_hbm, vall.at[r, pl.ds(0, mb)]), ("s", s_hbm, sv), ("ev", ev_hbm, evv),
@@ -86,15 +92,11 @@
     def pass_copy(s):
         return remote(val_block(s), val_block(s), pass_send.at[0], pass_recv.at[0], mate, j)
 
-    def peer_copy(phase, src, dst, peer):
-        return remote(src, dst, peer_send.at[phase], peer_recv.at[phase],
-                      peer // 2, group * 2 + lax.rem(peer, 2))
-
     def owner_copy(phase, src, dst, q, g):
         return remote(src, dst, own_send.at[phase], own_recv.at[phase],
                       q * (nj // 2) + group, g * 2 + plane)
 
-    groups = [lax.rem(group + k, nj // 2) for k in range(nj // 2)]
+    groups = [group] + far_groups
 
     def owner_each(q, g, away, here):
         if g is groups[0]:
@@ -123,8 +125,8 @@
         return remote(w0, w0, far_send.at[0], far_recv.at[0], r, g * 2 + plane)
 
     def all_send(phase, src_of, dst):
-        for p in peers:
-            peer_copy(phase, src_of(p), dst, p).start()
+        for s, p, col in peers:
+            remote(src_of(s, p), dst, peer_send.at[phase], peer_recv.at[phase], s, col).start()
 
     loads["c"].wait()
     loads["x"].wait()
@@ -196,7 +198,7 @@
     y0 = screen(w0[...])
     ysend0[0] = y0[:, :vh]
     ysend0[1] = y0[:, vh:]
-    all_send(0, lambda p: ysend0.at[lax.rem(p, 2)], yall0.at[me])
+    all_send(0, lambda s, p: ysend0.at[p], yall0.at[me])
     yall0[me] = ysend0[plane]
     arrived(call.at[:, pl.ds(0, nj - 1)], col_recv.at[0])
     condt[...] = call[...].reshape(np * nk, cw).T
@@ -222,12 +224,11 @@
 
     cond = call[...].reshape(np * nk, cw)
     esend[...] = jnp.dot(cond, x1t, preferred_element_type=F32).astype(BF16).reshape(esend.shape)
-    all_send(1, lambda p: esend.at[p], erecv.at[plane * nr + r])
+    all_send(1, lambda s, p: esend.at[s * 2 + p], erecv.at[plane * nr + r])
     erecv[plane * nr + r] = esend[me]
     kz0[plane] = k0t.astype(BF16)
 
-    other = group * 2 + 1 - plane
-    swap = remote(kz0.at[plane], kz0.at[plane], mate_send.at[0], mate_recv.at[0], r, other)
+    swap = remote(kz0.at[plane], kz0.at[plane], mate_send.at[0], mate_recv.at[0], r, across)
     swap.start()
     sent(yall0.at[pl.ds(0, np - 1)], peer_send.at[0])
     arrived(erecv.at[pl.ds(0, np - 1)], peer_recv.at[1])
@@ -239,16 +240,18 @@
             total = total + erecv[h * nr + i].astype(F32)
         halves.append(total)
     ysend1[...] = screen(jnp.concatenate(halves, axis=1).astype(BF16))
-    def cross(s, p):
-        return remote(ysend1, yall1.at[me], last_send.at[0],
-                      last_recv.at[r // 2 * 2 + plane], s, group * 2 + p)
+    from_slot = last_recv.at[r // 2 * 2 + plane]
+
+    def cross(s, col):
+        return remote(ysend1, yall1.at[me], last_send.at[0], from_slot, s, col)
 
     def hand(src, p):
         return remote(src, yall1.at[p], hand_send.at[0], hand_recv.at[0], mate, j)
 
-    others = ([(s, p) for s in chips for p in (1 - plane, plane)] + [(r, 1 - plane)])
-    for s, p in others:
-        cross(s, p).start()
+    for s in chips:
+        for p, col in planes:
+            cross(s, col).start()
+    cross(r, across).start()
     hand(ysend1, me).start()
     yall1[me] = ysend1[...]
     arrived(kz0.at[1 - plane], mate_recv.at[0])
@@ -257,7 +260,7 @@
     out_ref[0] = energy * (energy * xv[0] + k0)
     swap.wait_send()
     sent(erecv.at[pl.ds(0, np - 1)], peer_send.at[1])
-    sources = ([(lax.rem(r + nr - 2 * k, nr), p) for k in range(1, nr // 2)
+    sources = ([(rows[nr - 2 * k], p) for k in range(1, nr // 2)
                 for p in (1 - plane, plane)])
     for s, p in [(r, 1 - plane)] + sources:
         block = yall1.at[s * 2 + p]

time: 30.8 us -> 30.7 us (level)
  no operation moved by 1% of the time
where the time goes in v9:
time: 30.7 us; the launch traced here: 30.3 us
  Pallas kernels  29.7 us (97%)
  local copies, waits for them, and re-layouts  0.66 us (2%)
    pallas_call x1, Pallas kernels, fused(): pl.pallas_call(functools.partial(kernel, nr, nj), out_shape=pltpu.VMEM(tr...  29.7 us
    unnamed x1, local copies, waits for them, and re-layouts  0.66 us

profile of v9, /device:TPU:0, one launch (start us, length us, event | category | flops | bytes accessed | tf_op | source)
XLA Modules:
  0.0 30.3 jit_solution(8486506968668399424)
XLA Ops:
  0.0 29.7 %shard_map.64 = f32[1,256,128]{2,1,0:T(8,128)S(1)} custom-call(f32[1,256,128]{2,1,0:T(8,128)} %x_hbm.1, bf16[96,192]{1,0:T(8,128)(2,1)} %s_hbm.1, bf16[96,256]{1,0:T(8,128)(2,1)} %v_hbm.1, bf16[4,48,128]{2,1,0:T(8,128)(2,1)} %bitcast.3, f32[1,256]{1,0:T(1,128)} %bitcast.5, f32[1,1024]{1,0:T(1,128)} %bitcast.4), custom_call_target="tpu_custom_call" | custom-call | tf_op jit(solution)/shard_map/pallas_call | solution.py:327
  29.7 0.7 %copy.8 = f32[1,256,128]{2,1,0:T(8,128)} copy(f32[1,256,128]{2,1,0:T(8,128)S(1)} %shard_map.64) | data formatting | bytes 262144

commit v10 on v9

--- a/solution.py
+++ b/solution.py
@@ -133,6 +133,10 @@
     first = dot_nt(cv[...].reshape(nb, cw), xv[0].astype(BF16))
     asend[...] = first.astype(BF16).reshape(asend.shape)
 
+    if mb < LANES:
+        for i in range(nr):
+            vall[i, pl.ds(mb, LANES - mb)] = jnp.zeros((LANES - mb, nv), BF16)
+
     pl.semaphore_wait(barrier, greeted)
     owner_send(0, asend, arecv, groups[:1])
     for s in chips:
@@ -152,14 +156,6 @@
     for s in col_peers:
         remote(c_hbm, call.at[:, j], col_send.at[0], col_recv.at[0], r, s).start()
 
-    if mb < LANES:
-        for i in range(nr):
-            vall[i, pl.ds(mb, LANES - mb)] = jnp.zeros((LANES - mb, nv), BF16)
-    for name in ("ev", "ec", "call"):
-        loads[name].wait()
-    evb[...] = jnp.broadcast_to(evv[...], (LANES, nv)).T
-    ec = ecv[:, pl.ds(pl.multiple_of(r * cw, cw), cw)]
-
     def screen(w):
         allv = vall[...].reshape(nr * LANES, nv)
         inner = dot_nt(w, allv)
@@ -168,9 +164,6 @@
              for i in range(nr)], axis=1)
         return jnp.dot(tile, allv, preferred_element_type=F32).astype(BF16)
 
-    mine = pl.ds(pl.multiple_of(plane * vh, vh), vh)
-    b1t[...] = ((ec - evb[mine, :]) * xv[0, mine, :]).T
-
     @pl.when(holds)
     def _():
         arrived(arecv.at[pl.ds(0, nr - 1)], own_recv.at[0])
@@ -200,6 +193,12 @@
     ysend0[1] = y0[:, vh:]
     all_send(0, lambda s, p: ysend0.at[p], yall0.at[me])
     yall0[me] = ysend0[plane]
+    for name in ("ev", "ec", "call"):
+        loads[name].wait()
+    evb[...] = jnp.broadcast_to(evv[...], (LANES, nv)).T
+    ec = ecv[:, pl.ds(pl.multiple_of(r * cw, cw), cw)]
+    mine = pl.ds(pl.multiple_of(plane * vh, vh), vh)
+    b1t[...] = ((ec - evb[mine, :]) * xv[0, mine, :]).T
     arrived(call.at[:, pl.ds(0, nj - 1)], col_recv.at[0])
     condt[...] = call[...].reshape(np * nk, cw).T
     for s in chips:

time: 30.7 us -> 30.7 us (level)
  no operation moved by 1% of the time
where the time goes in v10:
time: 30.7 us; the launch traced here: 30.3 us
  Pallas kernels  29.7 us (97%)
  local copies, waits for them, and re-layouts  0.66 us (2%)
    pallas_call x1, Pallas kernels, fused(): pl.pallas_call(functools.partial(kernel, nr, nj), out_shape=pltpu.VMEM(tr...  29.7 us
    unnamed x1, local copies, waits for them, and re-layouts  0.66 us

profile of v10, /device:TPU:0, one launch (start us, length us, event | category | flops | bytes accessed | tf_op | source)
XLA Modules:
  0.0 30.3 jit_solution(15770107758832349541)
XLA Ops:
  0.0 29.7 %shard_map.64 = f32[1,256,128]{2,1,0:T(8,128)S(1)} custom-call(f32[1,256,128]{2,1,0:T(8,128)} %x_hbm.1, bf16[96,192]{1,0:T(8,128)(2,1)} %s_hbm.1, bf16[96,256]{1,0:T(8,128)(2,1)} %v_hbm.1, bf16[4,48,128]{2,1,0:T(8,128)(2,1)} %bitcast.3, f32[1,256]{1,0:T(1,128)} %bitcast.5, f32[1,1024]{1,0:T(1,128)} %bitcast.4), custom_call_target="tpu_custom_call" | custom-call | tf_op jit(solution)/shard_map/pallas_call | solution.py:326
  29.7 0.7 %copy.8 = f32[1,256,128]{2,1,0:T(8,128)} copy(f32[1,256,128]{2,1,0:T(8,128)S(1)} %shard_map.64) | data formatting | bytes 262144

commit v11 on v10

--- a/solution.py
+++ b/solution.py
@@ -137,13 +137,6 @@
         for i in range(nr):
             vall[i, pl.ds(mb, LANES - mb)] = jnp.zeros((LANES - mb, nv), BF16)
 
-    pl.semaphore_wait(barrier, greeted)
-    owner_send(0, asend, arecv, groups[:1])
-    for s in chips:
-        val_copy(s).start()
-    loads["v"].wait()
-    pass_copy(r).start()
-
     loads["s"].wait()
     scr = sv[...].astype(F32)
     scr = jnp.concatenate([scr, jnp.zeros((LANES - mb, nb), F32)], axis=0)
@@ -152,6 +145,14 @@
         scr = jnp.concatenate([scr, jnp.zeros((LANES, wide - nb), F32)], axis=1)
     scr = scr.T
     st[...] = scr[:nb].astype(BF16).reshape(st.shape)
+
+    pl.semaphore_wait(barrier, greeted)
+    owner_send(0, asend, arecv, groups[:1])
+    for s in chips:
+        val_copy(s).start()
+    loads["v"].wait()
+    pass_copy(r).start()
+
     owner_send(1, st, sall, groups[1:] + groups[:1])
     for s in col_peers:
         remote(c_hbm, call.at[:, j], col_send.at[0], col_recv.at[0], r, s).start()

time: 30.7 us -> 30.7 us (level)
  no operation moved by 1% of the time
where the time goes in v11:
time: 30.7 us; the launch traced here: 30.3 us
  Pallas kernels  29.7 us (97%)
  local copies, waits for them, and re-layouts  0.66 us (2%)
    pallas_call x1, Pallas kernels, fused(): pl.pallas_call(functools.partial(kernel, nr, nj), out_shape=pltpu.VMEM(tr...  29.7 us
    unnamed x1, local copies, waits for them, and re-layouts  0.66 us

profile of v11, /device:TPU:0, one launch (start us, length us, event | category | flops | bytes accessed | tf_op | source)
XLA Modules:
  0.0 30.3 jit_solution(1900144950637622535)
XLA Ops:
  0.0 29.7 %shard_map.64 = f32[1,256,128]{2,1,0:T(8,128)S(1)} custom-call(f32[1,256,128]{2,1,0:T(8,128)} %x_hbm.1, bf16[96,192]{1,0:T(8,128)(2,1)} %s_hbm.1, bf16[96,256]{1,0:T(8,128)(2,1)} %v_hbm.1, bf16[4,48,128]{2,1,0:T(8,128)(2,1)} %bitcast.3, f32[1,256]{1,0:T(1,128)} %bitcast.5, f32[1,1024]{1,0:T(1,128)} %bitcast.4), custom_call_target="tpu_custom_call" | custom-call | tf_op jit(solution)/shard_map/pallas_call | solution.py:327
  29.7 0.7 %copy.8 = f32[1,256,128]{2,1,0:T(8,128)} copy(f32[1,256,128]{2,1,0:T(8,128)S(1)} %shard_map.64) | data formatting | bytes 262144
